TPU v7x, 32 devices: a whole 2x2x4 slice. The times are simulated.
32 devices in a mesh: dp: 16 (over z, x, core), mp: 2 (over y).
Axes of the slice: x: 2, y: 2, z: 4, core: 2. Of those that a mesh axis runs over, the one named last changes fastest.
Arguments:
- tokens: bfloat16 [32, 788, 768], P(('dp', 'mp')), may hold values from -6 to 6
- cotangent: float32 [32, 788, 768], P(('dp', 'mp')), as said below
- rel_index: int32 [197, 197], replicated, may hold values from 0 to 731
- attn_owner: int32 [144], replicated, may hold values from 0 to 159, as said below
- mlp_owner: int32 [144], replicated, may hold values from 0 to 143, as said below
- attn_state: float32 [160, 7, 128, 128], P(('dp', 'mp')), as said below
- mlp_state: float32 [2, 144, 7, 128, 128], P('mp', 'dp'), as said below
- vec_param: float32 [10, 768], replicated
- vec_moments: float32 [2, 10, 768], replicated
- rel_table: float32 [12, 732], replicated, may hold values from -3 to 3
- rel_table_moments: float32 [2, 12, 732], replicated
- up_bias: float32 [3072], replicated, may hold values from -1 to 1
- up_bias_moments: float32 [2, 3072], replicated
Outputs:
- output: bfloat16 [32, 788, 768], P(('dp', 'mp'))
- input_grad: float32 [32, 788, 768], P(('dp', 'mp'))
- attn_update: float32 [160, 5, 128, 128], P(('dp', 'mp'))
- attn_copy: bfloat16 [160, 128, 128], P(('dp', 'mp'))
- mlp_update: float32 [2, 144, 5, 128, 128], P('mp', 'dp')
- mlp_copy: bfloat16 [2, 144, 128, 128], P('mp', 'dp')
- vector_update: float32 [4, 10, 768], replicated
- table_update: float32 [4, 12, 732], replicated
- up_bias_update: float32 [4, 3072], replicated
Inputs may be any that keep to these rules, and one draw needn't show every extreme that they name: `cotangent`: independent normal entries with deviation (25216)^-0.5. `attn_owner`: distinct slots, one for each attention tile; slots that no tile names stay empty. `mlp_owner`: distinct slots, one for each feed-forward tile of a part, the same list for every part; slots that no tile names stay empty. `attn_state`: channels 3 and 4 are symmetric positive definite, channels 5 and 6 orthogonal. `mlp_state`: channels 3 and 4 are symmetric positive definite, channels 5 and 6 orthogonal.
All inputs are finite; a program needn't handle non-finite values.
Results may differ from a plain program's by a relative error of at most 0.028.
Values may be sent and summed in bfloat16 or wider, within the bound.
A program may use at most 192 MiB of HBM per device.

v0:
```python
from functools import partial
import math

import jax
import jax.numpy as jnp
from jax import lax
from jax.sharding import PartitionSpec as P

D = 768
H = 12
HD = 64
FF = 3072
NPOS = 197
B = 128
STEP = 5


precise = lax.Precision.HIGHEST
ln_eps = 1e-06
beta_one = 0.9
beta_two = 0.95
beta_stat = 0.95
adam_eps = 1e-08
matrix_rate = 0.05
vector_rate = 0.2
decay_rate = 0.05


def norm_parts(values):
    centered = values - jnp.mean(values, axis=-1, keepdims=True)
    inv_std = lax.rsqrt(jnp.mean(centered * centered, axis=-1, keepdims=True) + ln_eps)
    return (centered * inv_std, inv_std)


def norm_back(grad_normed, scaled, inv_std, gain_row):
    tangent = grad_normed * gain_row
    return inv_std * (
        tangent
        - jnp.mean(tangent, axis=-1, keepdims=True)
        - scaled * jnp.mean(tangent * scaled, axis=-1, keepdims=True)
    )


def gelu_slope(values):
    cumulative = 0.5 * (1.0 + lax.erf(values * (1.0 / math.sqrt(2.0))))
    density = jnp.exp(-0.5 * values * values) * (1.0 / math.sqrt(2.0 * math.pi))
    return cumulative + values * density


def positions(segment_ids):
    row_ids = jnp.arange(segment_ids.shape[0], dtype=jnp.int32)
    same_label = segment_ids[:, None] == segment_ids[None, :]
    first_row = jnp.min(
        jnp.where(same_label, row_ids[None, :], jnp.int32(segment_ids.shape[0])), axis=1
    )
    return row_ids - first_row


def split_heads(matrix):
    return matrix.reshape(matrix.shape[0], H, HD).transpose(1, 0, 2)


def join_heads(stacked):
    return stacked.transpose(1, 0, 2).reshape(stacked.shape[1], H * HD)


def pair_groups(rel_index):
    pair_total = rel_index.shape[0] * rel_index.shape[1]
    group_rows = 8 * rel_index.shape[0]
    group_count = (pair_total + group_rows - 1) // group_rows
    padding = jnp.full((group_count * group_rows - pair_total,), -1, jnp.int32)
    return jnp.concatenate([rel_index.reshape(-1), padding]).reshape(group_count, group_rows)


def table_lookup(rel_table, grouped):

    def one_group(indices):
        onehot = (
            indices[:, None] == jnp.arange(rel_table.shape[1], dtype=jnp.int32)[None, :]
        ).astype(jnp.float32)
        return jnp.dot(rel_table, onehot.T, precision=precise)

    looked = lax.map(one_group, grouped)
    return looked.transpose(1, 0, 2).reshape(rel_table.shape[0], -1)


def table_accumulate(grid_flat, grouped, rel_total):
    head_count = grid_flat.shape[0]
    group_count = grouped.shape[0]
    group_rows = grouped.shape[1]
    padded = jnp.pad(grid_flat, ((0, 0), (0, group_count * group_rows - grid_flat.shape[1])))
    stacked = padded.reshape(head_count, group_count, group_rows).transpose(1, 0, 2)

    def one_group(running, members):
        indices, values = members
        onehot = (indices[:, None] == jnp.arange(rel_total, dtype=jnp.int32)[None, :]).astype(
            jnp.float32
        )
        return (running + jnp.dot(values, onehot, precision=precise), None)

    return lax.scan(one_group, jnp.zeros((head_count, rel_total), jnp.float32), (grouped, stacked))[
        0
    ]


def head_scores(q_head, k_head, bias_grid, position, same_image):
    bias_head = bias_grid[position][:, position]
    scores = (
        jnp.dot(q_head, k_head.T, preferred_element_type=jnp.float32) * HD ** (-0.5) + bias_head
    )
    return jnp.where(same_image, scores, -1e30)


def attention_forward(q_seq, k_seq, v_seq, seg_ids, bias_grids):
    position = positions(seg_ids)
    same_image = seg_ids[:, None] == seg_ids[None, :]

    def one_head(members):
        q_head, k_head, v_head, bias_grid = members
        masked = head_scores(q_head, k_head, bias_grid, position, same_image)
        row_top = jnp.max(masked, axis=1, keepdims=True)
        exp_scores = jnp.exp(masked - row_top)
        row_total = jnp.sum(exp_scores, axis=1, keepdims=True)
        attn_probs = exp_scores / row_total
        mixed_head = jnp.dot(
            attn_probs.astype(jnp.bfloat16), v_head, preferred_element_type=jnp.float32
        )
        return (mixed_head, (row_top + jnp.log(row_total))[:, 0])

    mixed_heads, log_total = lax.map(
        one_head, (split_heads(q_seq), split_heads(k_seq), split_heads(v_seq), bias_grids)
    )
    return (join_heads(mixed_heads), log_total)


def attention_backward(q_seq, k_seq, v_seq, seg_ids, log_total, grad_mixed, bias_grids):
    position = positions(seg_ids)
    same_image = seg_ids[:, None] == seg_ids[None, :]
    place_onehot = (position[:, None] == jnp.arange(NPOS, dtype=jnp.int32)[None, :]).astype(
        jnp.float32
    )
    onehot_low = place_onehot.astype(jnp.bfloat16)

    def one_head(members):
        q_head, k_head, v_head, bias_grid, log_head, grad_head = members
        masked = head_scores(q_head, k_head, bias_grid, position, same_image)
        attn_probs = jnp.exp(masked - log_head[:, None])
        grad_values = jnp.dot(
            attn_probs.astype(jnp.bfloat16).T, grad_head, preferred_element_type=jnp.float32
        )
        grad_probs = jnp.dot(grad_head, v_head.T, preferred_element_type=jnp.float32)
        row_dot = jnp.sum(attn_probs * grad_probs, axis=1, keepdims=True)
        grad_scores = (attn_probs * (grad_probs - row_dot)).astype(jnp.bfloat16)
        grad_queries = jnp.dot(grad_scores, k_head, preferred_element_type=jnp.float32) * HD ** (
            -0.5
        )
        grad_keys = jnp.dot(grad_scores.T, q_head, preferred_element_type=jnp.float32) * HD ** (
            -0.5
        )
        by_column = jnp.dot(grad_scores, onehot_low, preferred_element_type=jnp.float32)
        grid_grad = jnp.dot(place_onehot.T, by_column, precision=precise)
        return (grad_queries, grad_keys, grad_values, grid_grad)

    heads_out = lax.map(
        one_head,
        (
            split_heads(q_seq),
            split_heads(k_seq),
            split_heads(v_seq),
            bias_grids,
            log_total,
            split_heads(grad_mixed),
        ),
    )
    return (
        join_heads(heads_out[0]),
        join_heads(heads_out[1]),
        join_heads(heads_out[2]),
        heads_out[3],
    )


def cholesky_orth(product):
    gram = jnp.einsum("sji,sjk->sik", product, product, precision=precise)
    factor = jnp.linalg.cholesky(gram)
    solved = jax.vmap(partial(jax.scipy.linalg.solve_triangular, lower=True))(
        factor, jnp.swapaxes(product, 1, 2)
    )
    return jnp.swapaxes(solved, 1, 2)


def soap_update(grads, state, step_number):
    weight = state[:, 0]
    first_moment = state[:, 1]
    second_moment = state[:, 2]
    left_stat = state[:, 3]
    right_stat = state[:, 4]
    left_basis = state[:, 5]
    right_basis = state[:, 6]
    new_left = beta_stat * left_stat + (1.0 - beta_stat) * jnp.einsum(
        "sij,skj->sik", grads, grads, precision=precise
    )
    new_right = beta_stat * right_stat + (1.0 - beta_stat) * jnp.einsum(
        "sji,sjk->sik", grads, grads, precision=precise
    )
    left_orth = cholesky_orth(jnp.einsum("sij,sjk->sik", new_left, left_basis, precision=precise))
    right_orth = cholesky_orth(
        jnp.einsum("sij,sjk->sik", new_right, right_basis, precision=precise)
    )
    half_turn = jnp.einsum("sji,sjk->sik", left_orth, grads, precision=precise)
    rotated = jnp.einsum("sij,sjk->sik", half_turn, right_orth, precision=precise)
    new_first = beta_one * first_moment + (1.0 - beta_one) * rotated
    new_second = beta_two * second_moment + (1.0 - beta_two) * rotated * rotated
    fix_one = 1.0 - beta_one**step_number
    fix_two = 1.0 - beta_two**step_number
    normalized = new_first / fix_one / (jnp.sqrt(new_second / fix_two) + adam_eps)
    back_half = jnp.einsum("sij,sjk->sik", left_orth, normalized, precision=precise)
    update = jnp.einsum("sij,skj->sik", back_half, right_orth, precision=precise)
    new_weight = weight - matrix_rate * (update + decay_rate * weight)
    return jnp.stack([new_weight, new_first, new_second, left_orth, right_orth], axis=1)


def adam_vector(grads, param, moments, step_number):
    new_first = beta_one * moments[0] + (1.0 - beta_one) * grads
    new_second = beta_two * moments[1] + (1.0 - beta_two) * grads * grads
    fix_one = 1.0 - beta_one**step_number
    fix_two = 1.0 - beta_two**step_number
    new_param = param - vector_rate * (new_first / fix_one) / (
        jnp.sqrt(new_second / fix_two) + adam_eps
    )
    return jnp.stack([grads, new_param, new_first, new_second])


def body(
    tokens,
    cotangent,
    rel_index,
    attn_owner,
    mlp_owner,
    attn_state,
    mlp_state,
    vec_param,
    vec_moments,
    rel_table,
    rel_table_moments,
    up_bias,
    up_bias_moments,
):
    seq_count = tokens.shape[0]
    seq_len = tokens.shape[1]
    row_count = seq_count * seq_len
    tile_count = D // B
    segments = (jnp.arange(seq_len, dtype=jnp.int32) // NPOS)[None, :]
    attn_gathered = lax.all_gather(
        attn_state[:, 0].astype(jnp.bfloat16), ("dp", "mp"), axis=0, tiled=True
    )
    attn_weights = (
        attn_gathered[attn_owner]
        .reshape(4, tile_count, tile_count, B, B)
        .transpose(0, 1, 3, 2, 4)
        .reshape(4, D, D)
    )
    mlp_gathered = lax.all_gather(mlp_state[0, :, 0].astype(jnp.bfloat16), "dp", axis=0, tiled=True)
    mlp_blocks = mlp_gathered[mlp_owner]
    half_blocks = mlp_blocks.shape[0] // 2
    local_tiles = half_blocks // tile_count
    local_width = local_tiles * B
    up_weight = (
        mlp_blocks[:half_blocks]
        .reshape(tile_count, local_tiles, B, B)
        .transpose(0, 2, 1, 3)
        .reshape(D, local_width)
    )
    down_weight = (
        mlp_blocks[half_blocks:]
        .reshape(local_tiles, tile_count, B, B)
        .transpose(0, 2, 1, 3)
        .reshape(local_width, D)
    )
    grouped = pair_groups(rel_index)
    bias_grids = table_lookup(rel_table, grouped)[:, : NPOS * NPOS].reshape(H, NPOS, NPOS)
    inputs = tokens.reshape(row_count, D).astype(jnp.float32)
    scaled_one, inv_one = norm_parts(inputs)
    normed_one = (scaled_one * vec_param[0] + vec_param[1]).astype(jnp.bfloat16)
    merged_weight = attn_weights[:3].transpose(1, 0, 2).reshape(D, 3 * D)
    qkv_bias = jnp.concatenate([vec_param[2], jnp.zeros((D,), jnp.float32), vec_param[3]])
    projected = (
        jnp.dot(normed_one, merged_weight, preferred_element_type=jnp.float32) + qkv_bias
    ).astype(jnp.bfloat16)
    queries = projected[:, :D].reshape(seq_count, seq_len, D)
    keys_all = projected[:, D : 2 * D].reshape(seq_count, seq_len, D)
    values_all = projected[:, 2 * D :].reshape(seq_count, seq_len, D)

    def forward_seq(members):
        return attention_forward(members[0], members[1], members[2], members[3], bias_grids)

    mixed_all, log_total = lax.map(forward_seq, (queries, keys_all, values_all, segments))
    attended = mixed_all.reshape(row_count, D).astype(jnp.bfloat16)
    branch = jnp.dot(attended, attn_weights[3], preferred_element_type=jnp.float32) + vec_param[4]
    middle = inputs + vec_param[5] * branch
    scaled_two, inv_two = norm_parts(middle)
    normed_two = (scaled_two * vec_param[6] + vec_param[7]).astype(jnp.bfloat16)
    upstream = cotangent.reshape(row_count, D)
    grad_summed = (vec_param[9] * upstream).astype(jnp.bfloat16)
    group_rows = lax.all_gather(normed_two, "mp", axis=0, tiled=True)
    part_index = lax.axis_index("mp")
    local_bias = lax.dynamic_slice_in_dim(up_bias, part_index * local_width, local_width)
    hidden = jnp.dot(group_rows, up_weight, preferred_element_type=jnp.float32) + local_bias
    activated = jax.nn.gelu(hidden, approximate=False).astype(jnp.bfloat16)
    row_piece = activated
    summed = (
        lax.psum_scatter(
            jnp.dot(row_piece, down_weight, preferred_element_type=jnp.float32).astype(
                jnp.bfloat16
            ),
            "mp",
            scatter_dimension=0,
            tiled=True,
        ).astype(jnp.float32)
        + vec_param[8]
    )
    group_grad = lax.all_gather(grad_summed, "mp", axis=0, tiled=True)
    grad_hidden = (
        jnp.dot(group_grad, down_weight.T, preferred_element_type=jnp.float32) * gelu_slope(hidden)
    ).astype(jnp.bfloat16)
    grad_down = jnp.dot(activated.T, group_grad, preferred_element_type=jnp.float32)
    grad_up = jnp.dot(group_rows.T, grad_hidden, preferred_element_type=jnp.float32)
    local_bias_grad = jnp.sum(grad_hidden.astype(jnp.float32), axis=0)
    bias_grad_full = lax.dynamic_update_slice_in_dim(
        jnp.zeros((FF,), jnp.float32), local_bias_grad, part_index * local_width, 0
    )
    row_piece = grad_hidden
    grad_normed_two = lax.psum_scatter(
        jnp.dot(row_piece, up_weight.T, preferred_element_type=jnp.float32).astype(jnp.bfloat16),
        "mp",
        scatter_dimension=0,
        tiled=True,
    ).astype(jnp.float32)
    output = (middle + vec_param[9] * summed).astype(jnp.bfloat16).reshape(seq_count, seq_len, D)
    gamma_two_grad = jnp.sum(upstream * summed, axis=0)
    out_bias_grad = jnp.sum(grad_summed.astype(jnp.float32), axis=0)
    ln_two_gain = jnp.sum(grad_normed_two * scaled_two, axis=0)
    ln_two_bias = jnp.sum(grad_normed_two, axis=0)
    grad_middle = upstream + norm_back(grad_normed_two, scaled_two, inv_two, vec_param[6])
    grad_branch = (vec_param[5] * grad_middle).astype(jnp.bfloat16)
    gamma_one_grad = jnp.sum(grad_middle * branch, axis=0)
    proj_bias_grad = jnp.sum(grad_branch.astype(jnp.float32), axis=0)
    grad_proj = jnp.dot(attended.T, grad_branch, preferred_element_type=jnp.float32)
    grad_attended = jnp.dot(
        grad_branch, attn_weights[3].T, preferred_element_type=jnp.float32
    ).astype(jnp.bfloat16)

    def backward_seq(members):
        return attention_backward(
            members[0], members[1], members[2], members[3], members[4], members[5], bias_grids
        )

    grad_q, grad_k, grad_v, grid_grad = lax.map(
        backward_seq,
        (
            queries,
            keys_all,
            values_all,
            segments,
            log_total,
            grad_attended.reshape(seq_count, seq_len, D),
        ),
    )
    grad_qkv = (
        jnp.concatenate([grad_q, grad_k, grad_v], axis=-1)
        .reshape(row_count, 3 * D)
        .astype(jnp.bfloat16)
    )
    grad_merged = jnp.dot(normed_one.T, grad_qkv, preferred_element_type=jnp.float32)
    qkv_bias_grad = jnp.sum(grad_qkv.astype(jnp.float32), axis=0)
    grad_normed_one = jnp.dot(grad_qkv, merged_weight.T, preferred_element_type=jnp.float32)
    ln_one_gain = jnp.sum(grad_normed_one * scaled_one, axis=0)
    ln_one_bias = jnp.sum(grad_normed_one, axis=0)
    grad_inputs = grad_middle + norm_back(grad_normed_one, scaled_one, inv_one, vec_param[0])
    table_grad = table_accumulate(
        jnp.sum(grid_grad, axis=0).reshape(H, NPOS * NPOS), grouped, rel_table.shape[1]
    )
    attn_grad = jnp.concatenate(
        [grad_merged.reshape(D, 3, D).transpose(1, 0, 2), grad_proj[None]], axis=0
    )
    attn_tiles = (
        attn_grad.reshape(4, tile_count, B, tile_count, B)
        .transpose(0, 1, 3, 2, 4)
        .reshape(-1, B, B)
    )
    attn_slot_total = attn_state.shape[0] * lax.axis_size("dp") * lax.axis_size("mp")
    attn_slots = jnp.zeros((attn_slot_total, B, B), jnp.float32).at[attn_owner].set(attn_tiles)
    attn_mine = lax.psum_scatter(attn_slots, ("dp", "mp"), scatter_dimension=0, tiled=True)
    attn_result = soap_update(attn_mine, attn_state, STEP)
    up_tiles = (
        grad_up.reshape(tile_count, B, local_tiles, B).transpose(0, 2, 1, 3).reshape(-1, B, B)
    )
    down_tiles = (
        grad_down.reshape(local_tiles, B, tile_count, B).transpose(0, 2, 1, 3).reshape(-1, B, B)
    )
    mlp_slot_total = mlp_state.shape[1] * lax.axis_size("dp")
    mlp_slots = (
        jnp.zeros((mlp_slot_total, B, B), jnp.float32)
        .at[mlp_owner]
        .set(jnp.concatenate([up_tiles, down_tiles], axis=0))
    )
    mlp_mine = lax.psum_scatter(mlp_slots, "dp", scatter_dimension=0, tiled=True)
    mlp_result = soap_update(mlp_mine, mlp_state[0], STEP)[None]
    vector_grad = jnp.stack(
        [
            ln_one_gain,
            ln_one_bias,
            qkv_bias_grad[:D],
            qkv_bias_grad[2 * D :],
            proj_bias_grad,
            gamma_one_grad,
            ln_two_gain,
            ln_two_bias,
            out_bias_grad,
            gamma_two_grad,
        ]
    )
    vector_total, table_total, bias_total = lax.psum(
        (vector_grad, table_grad, bias_grad_full), ("dp", "mp")
    )
    return (
        output,
        grad_inputs.reshape(seq_count, seq_len, D),
        attn_result,
        attn_result[:, 0].astype(jnp.bfloat16),
        mlp_result,
        mlp_result[:, :, 0].astype(jnp.bfloat16),
        adam_vector(vector_total, vec_param, vec_moments, STEP),
        adam_vector(table_total, rel_table, rel_table_moments, STEP),
        adam_vector(bias_total, up_bias, up_bias_moments, STEP),
    )


def solution(mesh):
    placed = (
        P(("dp", "mp"), None, None),
        P(("dp", "mp"), None, None),
        P(),
        P(),
        P(),
        P(("dp", "mp"), None, None, None),
        P("mp", "dp", None, None, None),
        P(),
        P(),
        P(),
        P(),
        P(),
        P(),
    )
    return jax.shard_map(
        body,
        mesh=mesh,
        in_specs=placed,
        out_specs=(
            P(("dp", "mp"), None, None),
            P(("dp", "mp"), None, None),
            P(("dp", "mp"), None, None, None),
            P(("dp", "mp"), None, None),
            P("mp", "dp", None, None, None),
            P("mp", "dp", None, None),
            P(),
            P(),
            P(),
        ),
        check_vma=False,
    )
```

profile of v0, /device:TPU:0, one launch (start us, length us, event | category | flops | bytes accessed | tf_op | source)
XLA Modules:
  0.0 1883.0 jit_solution(14014876325800085656)
XLA Ops:
  19.0 75.1 %while.74 = (s32[]{:T(128)}, f32[25,12,1576]{2,1,0:T(8,128)}, s32[25,1576]{1,0:T(8,128)S(1)}, f32[12,732]{1,0:T(8,128)S(1)}, s32[]{:T(128)}) while((s32[]{:T(128)}, f32[25,12,1576]{2,1,0:T(8,128)}, s32[25,1576]{1,0:T(8,128)S(1)}, f32[12,732]{1,0:T(8,128)S(1)}, s32[]{:T(128)}) %tuple.189), condition=%wide.region_3.4_spmd, body=%wide.region_2.3_spmd.sunk | while | flops 167276640 | bytes 161121 | solution.py:83
  94.1 4.1 copy.299
  109.6 10.5 gather_fusion.4
  120.2 6.6 copy.504
  132.4 8.3 slice.159
  140.8 6.0 copy.296
  146.8 6.2 add_convert_fusion
  168.1 187.4 %while.75 = (s32[]{:T(128)}, bf16[12,788,64]{1,2,0:T(8,128)(2,1)}, f32[12,788]{1,0:T(8,128)}, bf16[12,788,64]{2,1,0:T(8,128)(2,1)}, bf16[12,788,64]{2,1,0:T(8,12...) while((s32[]{:T(128)}, bf16[12,788,64]{1,2,0:T(8,128)(2,1)}, ...), condition=%wide.region_8.9_spmd.clone, body=%wide.region_5.8_spmd.clone.sunk | while | flops 165173712 | bytes 28934140 | solution.py:130
  369.1 10.1 gather_fusion.5
  387.5 15.1 all-gather.12.cloned.1.call-done
  406.3 27.0 %fusion.73 = (bf16[1576,1536]{1,0:T(8,128)(2,1)S(1)}, f32[1576,1536]{1,0:T(8,128)S(1)}) fusion(f32[1536]{0:T(1024)S(1)} %dynamic_slice.70, bf16[1576,768]{1,0:T(8,128)(2,1)} %reshape.527, bf16[96,8,12,128]{3,2,1,0:T(8,128)(2,1)} %bitcast.639), kind=kOutput, calls=%fused_computation.100 | convolution fusion | flops 3878019072 | bytes 19310592 | tf_op jit(solution)/shard_map/dot_general | solution.py:308
  433.3 7.5 convert_reduce_fusion
  440.9 5.3 convolution_convert_fusion
  446.2 6.4 fusion.257
  452.6 5.2 convolution_convert_fusion.1
  457.7 59.0 %fusion.242 = (bf16[792,768]{1,0:T(8,128)(2,1)S(1)}, bf16[792,768]{1,0:T(8,128)(2,1)S(1)}) fusion(bf16[1576,768]{1,0:T(8,128)(2,1)} %convolution_convert_fusion.1, bf16[1576,768]{1,0:T(8,128)(2,1)} %convolution_convert_fusion), kind=kCustom, calls=%all-reduce-scatter.2 | all-reduce-scatter fusion | flops 2433025 | bytes 7275008
  519.1 8.7 fusion.258
  529.1 6.7 reshape.451
  535.8 6.5 copy.337
  542.3 6.6 reshape.453
  548.9 5.7 copy.338
  555.0 7.1 concatenate.42
  564.8 7.2 concatenate.41
  572.0 5.6 multiply_reduce_fusion.1
  587.0 278.8 %while.77 = (s32[]{:T(128)}, bf16[12,788,64]{1,2,0:T(8,128)(2,1)}, bf16[12,788,64]{1,2,0:T(8,128)(2,1)}, bf16[12,788,64]{1,2,0:T(8,128)(2,1)}, f32[12,197,197]{2...) while((s32[]{:T(128)}, bf16[12,788,64]{1,2,0:T(8,128)(2,1)}, ...), condition=%wide.region_17.18_spmd.clone.clone, body=%wide.region_15.17_spmd.clone.clone.sunk | while | flops 1016744000 | bytes 54928680 | solution.py:164
  865.8 4.9 convert_reduce_fusion.1
  871.3 6.4 fusion.108
  884.9 4.2 reshape.456
  889.1 92.7 %while.76 = (s32[]{:T(128)}, f32[12,732]{1,0:T(8,128)S(1)}, f32[25,12,1576]{2,0,1:T(8,128)}, s32[25,1576]{1,0:T(8,128)}, s32[]{:T(128)}, /*index=5*/s32[]{:T(128)}) while((s32[]{:T(128)}, f32[12,732]{1,0:T(8,128)S(1)}, f32[25,12,1576]{2,0,1:T(8,128)}, s32[25,1576]{1,0:T(8,128)}, s32[]{:T(128)}, /*index=5*/s32[]{:T(128)}) %tuple.190), condition=%wide.region_39.44_spmd.clone, body=%wide.region_38.43_spmd.clone.sunk | while | flops 167294208 | bytes 316215 | solution.py:101
  983.1 8.8 pad_maximum_fusion
  991.9 4.8 broadcast_in_dim.170
  996.8 26.3 %scatter_fusion.1 = f32[144,128,128]{2,1,0:T(8,128)} fusion(f32[144,128,128]{2,1,0:T(8,128)} %broadcast_in_dim.170, s32[144]{0:T(256)S(1)} %copy-done.74, f32[144,128,128]{2,1,0:T(8,128)} %pad_maximum_fusion), kind=kCustom, calls=%fused_computation.7 | custom fusion | bytes 28312128 | tf_op jit(solution)/shard_map/scatter | solution.py:405
  1023.8 8.7 convolution_bitcast_fusion.1
  1032.4 8.9 concatenate.38
  1048.1 9.8 maximum_bitcast_fusion
  1057.9 9.9 copy.318
  1067.8 5.3 broadcast_in_dim.166
  1073.1 26.4 %scatter_fusion = f32[160,128,128]{2,1,0:T(8,128)} fusion(f32[160,128,128]{2,1,0:T(8,128)} %broadcast_in_dim.166, s32[144]{0:T(256)S(1)} %copy-done.72, f32[144,128,128]{2,1,0:T(8,128)} %bitcast.598), kind=kCustom, calls=%fused_computation.6 | custom fusion | bytes 28312128 | tf_op jit(solution)/shard_map/scatter | solution.py:392
  1099.6 4.9 copy.505
  1117.7 103.7 %reduce-scatter.9.cloned.1.call-done = f32[9,128,128]{2,1,0:T(8,128)} async-done(((f32[144,128,128]{2,1,0:T(8,128)}), f32[9,128,128]{2,1,0:T(8,128)}) %reduce-scatter.9.cloned.1.call-update) | async-done | bytes 589840 | tf_op jit(solution)/shard_map/reduce_scatter | solution.py:407
  1227.4 105.7 %custom-call.21 = f32[9,128,128]{2,1,0:T(8,128)S(1)} custom-call(f32[9,128,128]{2,1,0:T(8,128)S(1)} %fusion.164), custom_call_target="Cholesky" | custom-call | tf_op jit(solution)/shard_map/jit(cholesky)/cholesky | solution.py:185
  1339.2 106.3 %custom-call.23 = f32[9,128,128]{2,1,0:T(8,128)S(1)} custom-call(f32[9,128,128]{2,1,0:T(8,128)} %fusion.160), custom_call_target="Cholesky" | custom-call | tf_op jit(solution)/shard_map/jit(cholesky)/cholesky | solution.py:185
  1447.4 88.4 %custom-call.24 = f32[9,1,128,128]{2,3,1,0:T(8,128)S(1)} custom-call(f32[9,1,128,128]{3,2,1,0:T(8,128)S(1)} %get-tuple-element.632), custom_call_target="InvertDiagBlocksLowerTriangular" | custom-call | tf_op jit(solution)/shard_map/vmap(jit(_solve_triangular))/triangular_solve | solution.py:186
  1535.8 89.4 %custom-call.22 = f32[9,1,128,128]{2,3,1,0:T(8,128)S(1)} custom-call(f32[9,1,128,128]{3,2,1,0:T(8,128)} %get-tuple-element.633), custom_call_target="InvertDiagBlocksLowerTriangular" | custom-call | tf_op jit(solution)/shard_map/vmap(jit(_solve_triangular))/triangular_solve | solution.py:186
  1645.4 60.4 %custom-call.17 = f32[5,128,128]{2,1,0:T(8,128)} custom-call(f32[5,128,128]{2,1,0:T(8,128)} %fusion.188), custom_call_target="Cholesky" | custom-call | tf_op jit(solution)/shard_map/jit(cholesky)/cholesky | solution.py:185
  1707.9 58.6 %custom-call.19 = f32[5,128,128]{2,1,0:T(8,128)S(1)} custom-call(f32[5,128,128]{2,1,0:T(8,128)S(1)} %fusion.184), custom_call_target="Cholesky" | custom-call | tf_op jit(solution)/shard_map/jit(cholesky)/cholesky | solution.py:185
  1767.0 49.3 %custom-call.20 = f32[5,1,128,128]{2,3,1,0:T(8,128)S(1)} custom-call(f32[5,1,128,128]{3,2,1,0:T(8,128)S(1)} %get-tuple-element.634), custom_call_target="InvertDiagBlocksLowerTriangular" | custom-call | tf_op jit(solution)/shard_map/vmap(jit(_solve_triangular))/triangular_solve | solution.py:186
  1817.0 49.1 %custom-call.18 = f32[5,1,128,128]{2,3,1,0:T(8,128)S(1)} custom-call(f32[5,1,128,128]{3,2,1,0:T(8,128)S(1)} %get-tuple-element.635), custom_call_target="InvertDiagBlocksLowerTriangular" | custom-call | tf_op jit(solution)/shard_map/vmap(jit(_solve_triangular))/triangular_solve | solution.py:186
  (961 shorter events, 791.2 us)
Async XLA Ops:
  7.2 102.4 %all-gather.8.cloned.1.call-start = ((), (), s32[]{:S(2)}) async-start(), calls=%async_computation.2 | async-start | bytes 5406720 | tf_op jit(solution)/shard_map/all_gather | solution.py:254
  8.9 356.6 %all-gather.14.cloned.1.call-start = ((), (), s32[]{:S(2)}) async-start(), calls=%async_computation.7 | async-start | bytes 3649536 | tf_op jit(solution)/shard_map/all_gather | solution.py:322
  10.7 136.1 %copy-start.66 = (f32[768]{0:T(1024)}, f32[768]{0:T(1024)S(1)}, u32[]{:S(2)}) copy-start(f32[768]{0:T(1024)S(1)} %get-tuple-element.523) | copy-start | bytes 9220
  10.7 136.1 %copy-start.75 = (f32[768]{0:T(1024)}, f32[768]{0:T(1024)S(1)}, u32[]{:S(2)}) copy-start(f32[768]{0:T(1024)S(1)} %get-tuple-element.522) | copy-start | bytes 9220
  11.3 5.1 copy-start.9
  14.3 354.8 %all-gather.10.cloned.1.call-start = ((), (), s32[]{:S(2)}) async-start(), calls=%async_computation.5 | async-start | bytes 5013504 | tf_op jit(solution)/shard_map/all_gather | solution.py:263
  16.3 386.4 %all-gather.12.cloned.1.call-start = ((), (), s32[]{:S(2)}) async-start(), calls=%async_computation.6 | async-start | bytes 3649536 | tf_op jit(solution)/shard_map/all_gather | solution.py:305
  16.6 130.2 %copy-start.58 = (f32[788]{0:T(1024)}, f32[788]{0:T(1024)S(1)}, u32[]{:S(2)}) copy-start(f32[788]{0:T(1024)S(1)} %broadcast_multiply_fusion.5) | copy-start | bytes 9460
  17.2 129.6 %copy-start.68 = (f32[788]{0:T(1024)}, f32[788]{0:T(1024)S(1)}, u32[]{:S(2)}) copy-start(f32[788]{0:T(1024)S(1)} %add_rsqrt_fusion.1) | copy-start | bytes 9460
  355.5 5.0 copy-start.34
  363.5 747.3 %all-reduce.10.cloned.1.call-start = ((), (), s32[]{:S(2)}) async-start(), calls=%async_computation.8 | async-start | bytes 221184 | tf_op jit(solution)/shard_map/psum | solution.py:423
  406.3 27.0 %copy-start.27 = (bf16[1576,768]{1,0:T(8,128)(2,1)S(1)}, bf16[1576,768]{1,0:T(8,128)(2,1)}, u32[]{:S(2)}) copy-start(bf16[1576,768]{1,0:T(8,128)(2,1)} %reshape.529) | copy-start | bytes 7262212
  433.3 19.3 %copy-start.80 = (bf16[1576,1536]{1,0:T(8,128)(2,1)}, bf16[1576,1536]{1,0:T(8,128)(2,1)S(1)}, u32[]{:S(2)}) copy-start(bf16[1576,1536]{1,0:T(8,128)(2,1)S(1)} %get-tuple-element.639) | copy-start | bytes 14524420
  433.3 7.6 copy-start.24
  440.9 5.3 copy-start.28
  516.7 11.1 copy-start.19
  516.7 11.1 copy-start.18
  516.8 38.2 %collective-permute-start.1 = (bf16[4,768]{1,0:T(4,128)(2,1)S(1)}, bf16[4,768]{1,0:T(4,128)(2,1)S(1)}, u32[]{:S(2)}, u32[]{:S(2)}) collective-permute-start(bf16[4,768]{1,0:T(4,128)(2,1)S(1)} %slice.229), channel_id=1, source_target_pairs={{0,1},{2,3},{4,5},{6,7},{8,9},{10,11},{12,13},{14,15},{16,17},{18,... | collective-permute-start | bytes 18440
  527.8 37.0 %collective-permute-start = (bf16[4,768]{1,0:T(4,128)(2,1)S(1)}, bf16[4,768]{1,0:T(4,128)(2,1)S(1)}, u32[]{:S(2)}, u32[]{:S(2)}) collective-permute-start(bf16[4,768]{1,0:T(4,128)(2,1)S(1)} %slice.228), channel_id=1, source_target_pairs={{0,1},{2,3},{4,5},{6,7},{8,9},{10,11},{12,13},{14,15},{16,17},{18,... | collective-permute-start | bytes 18440
  554.6 7.5 copy-start.5
  554.6 7.5 copy-start.42
  554.6 7.5 copy-start.45
  554.6 7.5 copy-start.47
  555.0 9.8 copy-start.53
  562.1 9.9 copy-start.55
  562.1 9.8 copy-start.57
  562.1 9.8 copy-start.65
  572.0 7.1 copy-start.61
  865.8 5.0 copy-start.14
  865.8 5.0 copy-start.15
  865.8 5.5 copy-start.23
  865.8 5.5 copy-start.59
  865.8 5.5 copy-start.67
  865.8 5.5 copy-start.69
  983.1 238.3 %reduce-scatter.9.cloned.1.call-start = ((), (), s32[]{:S(2)}) async-start(), calls=%async_computation.4 | async-start | bytes 10027008 | tf_op jit(solution)/shard_map/reduce_scatter | solution.py:407
  1023.1 616.4 %reduce-scatter.7.cloned.1.call-start = ((), (), s32[]{:S(2)}) async-start(), calls=%async_computation.3 | async-start | bytes 10813440 | tf_op jit(solution)/shard_map/reduce_scatter | solution.py:393
  1067.8 5.3 copy-start.72
  1099.6 5.6 copy-start.48
  1099.6 5.6 copy-start.43
  1099.6 5.7 copy-start.64
  1099.6 5.7 copy-start.8
  1099.6 5.7 copy-start.26
  1106.8 6.4 copy-start.40
  1106.8 8.8 copy-start.63
  1225.9 107.1 %copy-start.12 = (f32[9,128,128]{2,1,0:T(8,128)S(1)}, f32[9,128,128]{2,1,0:T(8,128)}, u32[]{:S(2)}) copy-start(f32[9,128,128]{2,1,0:T(8,128)} %reduce-scatter.9.cloned.1.call-done) | copy-start | bytes 1769476
  1639.6 66.2 %copy-start.13 = (f32[5,128,128]{2,1,0:T(8,128)S(1)}, f32[5,128,128]{2,1,0:T(8,128)}, u32[]{:S(2)}) copy-start(f32[5,128,128]{2,1,0:T(8,128)} %reduce-scatter.7.cloned.1.call-done) | copy-start | bytes 983044
  1705.8 60.7 %copy-start.39 = (pred[128,128]{1,0:T(8,128)(4,1)S(1)}, pred[128,128]{1,0:T(8,128)(4,1)}, u32[]{:S(2)}) copy-start(pred[128,128]{1,0:T(8,128)(4,1)} %iota_compare_fusion.13) | copy-start | bytes 49156
  1707.0 59.6 %copy-start.31 = (f32[5,128,128]{2,1,0:T(8,128)S(1)}, f32[5,128,128]{2,1,0:T(8,128)}, u32[]{:S(2)}) copy-start(f32[5,128,128]{2,1,0:T(8,128)} %custom-call.17) | copy-start | bytes 983044
  (119 other events, 302.6 us)
Sparse Core Ops, SparseCore 0:
  11.4 68.0 all-gather.7
  81.7 35.7 all-gather.13
  120.4 53.2 all-gather.9
  363.6 39.0 all-gather.11
  983.2 121.7 all-reduce.9
  1109.0 112.3 reduce-scatter.8
  1223.8 226.4 reduce-scatter.6
where the time goes:
time: 1900 us; the launch traced here: 1880 us
  other arithmetic  672 us (35%)
  local copies, waits for them, and re-layouts  567 us (30%)
  matrix products  442 us (23%)
  waiting for transfers between devices  119 us (6%)
  blocking collectives  59 us (3%)
    another operation x10, other arithmetic, cholesky_orth(): factor = jnp.linalg.cholesky(gram)  333 us
    another operation x7, other arithmetic, cholesky_orth(): jax.vmap(partial(jax.scipy.linalg.solve_triangular, lower=True))  277 us
    gather x72, local copies, waits for them, and re-layouts, head_scores(): bias_head = bias_grid[position][:, position]  157 us
    reduce_scatter x1, waiting for transfers between devices, body(): lax.psum_scatter(mlp_slots, 'dp', scatter_dimension=0, tiled=True)  104 us
    dot_general x25, matrix products, one_group(): return jnp.dot(rel_table, onehot.T, precision=precise)  74.4 us
    unnamed x1, blocking collectives  59 us
    unnamed x166, local copies, waits for them, and re-layouts  52.8 us
    dot_general x24, matrix products, head_scores(): jnp.dot(q_head, k_head.T, preferred_element_type=jnp.float32) * HD ** (-0.5)  47.6 us
  transfers between devices with their start and end apart: 9, of which 2 were waited for; matrix products, arithmetic and copies ran while one was open for 50% of the time, Pallas kernels for 0%

commit v1 on v0

v1 whole, which is shorter than its diff:
```python
from functools import partial
import math

import jax
import jax.numpy as jnp
from jax import lax
from jax.experimental import pallas as pl
from jax.experimental.pallas import tpu as pltpu
from jax.sharding import PartitionSpec as P

D = 768
H = 12
HD = 64
FF = 3072
NPOS = 197
NP = 208
NL = 256
B = 128
STEP = 5
T = D // B

f32 = jnp.float32
bf16 = jnp.bfloat16

ln_eps = 1e-06
beta_one = 0.9
beta_two = 0.95
beta_stat = 0.95
adam_eps = 1e-08
matrix_rate = 0.05
vector_rate = 0.2
decay_rate = 0.05

VMEM = pl.BlockSpec(memory_space=pltpu.VMEM)
SMEM = pl.BlockSpec(memory_space=pltpu.SMEM)
ANY = pl.BlockSpec(memory_space=pl.ANY)
LIMIT = 60 << 20


def shape(dims, kind):
    return jax.ShapeDtypeStruct(dims, kind)


def dot_nn(x, y):
    return lax.dot_general(x, y, (((1,), (0,)), ((), ())), preferred_element_type=f32)


def dot_nt(x, y):
    return lax.dot_general(x, y, (((1,), (1,)), ((), ())), preferred_element_type=f32)


def dot_tn(x, y):
    return lax.dot_general(x, y, (((0,), (0,)), ((), ())), preferred_element_type=f32)


def norm_parts(values):
    centered = values - jnp.mean(values, axis=-1, keepdims=True)
    inv_std = lax.rsqrt(jnp.mean(centered * centered, axis=-1, keepdims=True) + ln_eps)
    return (centered * inv_std, inv_std)


def norm_back(grad_normed, scaled, inv_std, gain_row):
    tangent = grad_normed * gain_row
    return inv_std * (
        tangent
        - jnp.mean(tangent, axis=-1, keepdims=True)
        - scaled * jnp.mean(tangent * scaled, axis=-1, keepdims=True)
    )


def lookup_kernel(idx_ref, table_ref, out_ref, spread):
    chunks = table_ref.shape[1] // B
    for h in range(H):
        for c in range(chunks):
            spread[h, c] = jnp.broadcast_to(table_ref[h : h + 1, c * B : (c + 1) * B], (8, B))

    @pl.loop(0, NP // 8)
    def _(jt):
        rows = pl.ds(pl.multiple_of(jt * 8, 8), 8)
        real = jt * 8 + lax.broadcasted_iota(jnp.int32, (8, B), 0) < NPOS
        for half in range(NL // B):
            lanes = slice(half * B, (half + 1) * B)
            idx = idx_ref[rows, lanes]
            low = jnp.bitwise_and(idx, B - 1)
            high = jnp.right_shift(idx, 7)
            for h in range(H):
                acc = jnp.take_along_axis(spread[h, 0], low, axis=1, mode="promise_in_bounds")
                for c in range(1, chunks):
                    part = jnp.take_along_axis(spread[h, c], low, axis=1, mode="promise_in_bounds")
                    acc = jnp.where(high == c, part, acc)
                out_ref[h, rows, lanes] = jnp.where(real, acc, -1e30)


def table_lookup(idx_t, table_pad):
    return pl.pallas_call(
        lookup_kernel,
        in_specs=[VMEM, VMEM],
        out_specs=VMEM,
        out_shape=shape((H, NP, NL), f32),
        scratch_shapes=[pltpu.VMEM((H, table_pad.shape[1] // B, 8, B), f32)],
        compiler_params=pltpu.CompilerParams(vmem_limit_bytes=LIMIT),
        name="table_lookup",
    )(idx_t, table_pad)


def accumulate_kernel(grid_ref, idx_ref, out_ref):
    chunks = out_ref.shape[0]
    out_ref[...] = jnp.zeros_like(out_ref)
    lo_rows = lax.broadcasted_iota(jnp.int32, (B, NL), 0)

    @pl.loop(0, NPOS)
    def _(j):
        values = grid_ref[:, j, :]
        values = jnp.concatenate([values, jnp.zeros((4, NL), f32)], axis=0)
        idx = idx_ref[pl.ds(j, 1), :]
        low = jnp.bitwise_and(idx, B - 1)
        high = jnp.right_shift(idx, 7)
        onehot = jnp.where(lo_rows == low, 1.0, 0.0).astype(bf16)
        first = values.astype(bf16)
        second = (values - first.astype(f32)).astype(bf16)
        rows = []
        for c in range(chunks):
            rows.append(jnp.where(high == c, values, 0.0))
        stacked = jnp.concatenate(rows, axis=0)
        first = stacked.astype(bf16)
        second = (stacked - first.astype(f32)).astype(bf16)
        got = dot_nt(jnp.concatenate([first, second], axis=0), onehot)
        for c in range(chunks):
            base = c * 16
            out_ref[c] += got[base : base + 16] + got[chunks * 16 + base : chunks * 16 + base + 16]


def table_accumulate(grid_t, idx_t, chunks):
    return pl.pallas_call(
        accumulate_kernel,
        in_specs=[VMEM, VMEM],
        out_specs=VMEM,
        out_shape=shape((chunks, 16, B), f32),
        compiler_params=pltpu.CompilerParams(vmem_limit_bytes=LIMIT),
        name="table_accumulate",
    )(grid_t, idx_t)


def attn_tile(weights, b):
    m = b // (T * T)
    r = lax.rem(b // T, T)
    c = lax.rem(b, T)
    return weights.at[
        m, pl.ds(pl.multiple_of(r * B, B), B), pl.ds(pl.multiple_of(c * B, B), B)
    ]


def pad_rows(x):
    return jnp.concatenate([x, jnp.zeros((NL - NP, x.shape[1]), x.dtype)], axis=0)


def forward_kernel(
    own, tok, slots, vec, bias, w, q, k, v, att, lse, mid, bra, n2, n1, sem
):
    imgs = q.shape[0]

    @pl.loop(0, own.shape[0])
    def _(b):
        pltpu.make_async_copy(slots.at[own[b]], attn_tile(w, b), sem).start()

    for img in range(imgs):
        x, _ = norm_parts(tok[img].astype(f32))
        n1[img * NP : (img + 1) * NP] = (x * vec[0:1] + vec[1:2]).astype(bf16)
    pltpu.make_async_copy(w, w, sem).wait()

    for m, (out, row, scale) in enumerate(((q, 2, HD**-0.5), (k, None, 1.0), (v, 3, 1.0))):
        for n in range(D // NL):
            lanes = slice(n * NL, (n + 1) * NL)
            part = dot_nn(n1[...], w[m, :, lanes])
            if row is not None:
                part = part + vec[row : row + 1, lanes]
            part = part.astype(bf16)
            if scale != 1.0:
                part = part * jnp.asarray(scale, bf16)
            for img in range(imgs):
                out[img, :, lanes] = part[img * NP : (img + 1) * NP]

    @pl.loop(0, imgs)
    def _(img):
        side = lax.broadcasted_iota(jnp.int32, (1, B), 1) // HD
        for pair in range(H // 2):
            lanes = slice(pair * B, (pair + 1) * B)
            k_pair = k[img, :, lanes]
            q_pair = pad_rows(q[img, :, lanes])
            v_turn = v[img, :, lanes].astype(f32).T.astype(bf16)
            mixed = []
            for sub in range(2):
                h = pair * 2 + sub
                q_one = jnp.where(side == sub, q_pair, jnp.zeros_like(q_pair))
                s = dot_nt(k_pair, q_one) + bias[h]
                top = jnp.max(s, axis=0, keepdims=True)
                e = jnp.exp(s - top)
                total = jnp.sum(e, axis=0, keepdims=True)
                o = dot_nn(v_turn[sub * HD : (sub + 1) * HD], e.astype(bf16))
                mixed.append(o * (1.0 / total))
                lse[img, h : h + 1] = top + jnp.log(total)
            both = jnp.concatenate(mixed, axis=0).T
            att[img, :, lanes] = both[:NP].astype(bf16)

    @pl.loop(0, imgs)
    def _(img):
        branch = dot_nn(att[img], w[3]) + vec[4:5]
        bra[img] = branch
        middle = tok[img].astype(f32) + vec[5:6] * branch
        mid[img] = middle
        x, _ = norm_parts(middle)
        n2[img] = (x * vec[6:7] + vec[7:8]).astype(bf16)


def forward_attention(tok, slots, own, vec, bias):
    imgs = tok.shape[0]
    big = shape((imgs, NP, D), bf16)
    wide = shape((imgs, NP, D), f32)
    return pl.pallas_call(
        forward_kernel,
        in_specs=[SMEM, VMEM, ANY, VMEM, VMEM],
        out_specs=[VMEM] * 9,
        out_shape=[
            shape((4, D, D), bf16),
            big,
            big,
            big,
            big,
            shape((imgs, H, NL), f32),
            wide,
            wide,
            big,
        ],
        scratch_shapes=[pltpu.VMEM((imgs * NP, D), bf16), pltpu.SemaphoreType.DMA(())],
        compiler_params=pltpu.CompilerParams(vmem_limit_bytes=LIMIT),
        name="forward_attention",
    )(own, tok, slots, vec, bias)


CH = 512


def mlp_kernel(
    parts,
    each,
    own,
    mid,
    bra,
    n2,
    cot,
    slots,
    vec,
    upb,
    out,
    gmid,
    gbra,
    sums,
    bgrad,
    tiles_out,
    w1,
    w2,
    gs,
    act,
    gh,
    summed,
    gn2,
    tiles,
    sem_in,
    sem_out,
):
    imgs = mid.shape[0]
    rows = imgs * NP
    chunks = FF // CH
    per = CH // B
    half = own.shape[0] // 2
    total = parts * half
    local = half // T

    def place(slot, p):
        return (slot // each) * (parts * each) + p * each + lax.rem(slot, each)

    @pl.loop(0, total)
    def _(b):
        p = b // half
        rest = lax.rem(b, half)
        r = rest // local
        c = p * local + lax.rem(rest, local)
        pltpu.make_async_copy(
            slots.at[place(own[rest], p)],
            w1.at[
                c // per,
                pl.ds(pl.multiple_of(r * B, B), B),
                pl.ds(pl.multiple_of(lax.rem(c, per) * B, B), B),
            ],
            sem_in,
        ).start()
        r2 = p * local + rest // T
        c2 = lax.rem(rest, T)
        pltpu.make_async_copy(
            slots.at[place(own[half + rest], p)],
            w2.at[pl.ds(pl.multiple_of(r2 * B, B), B), pl.ds(pl.multiple_of(c2 * B, B), B)],
            sem_in,
        ).start()

    for img in range(imgs):
        gs[img * NP : (img + 1) * NP] = (vec[9:10] * cot[img]).astype(bf16)
    summed[...] = jnp.zeros_like(summed)
    gn2[...] = jnp.zeros_like(gn2)
    pltpu.make_async_copy(w1, w1, sem_in).wait()
    pltpu.make_async_copy(w2, w2, sem_in).wait()

    @pl.loop(0, chunks)
    def _(c):
        span = pl.ds(pl.multiple_of(c * CH, CH), CH)
        bias_sum = jnp.zeros((1, CH), f32)
        for rb in range(imgs // 2):
            block = slice(rb * 2 * NP, (rb + 1) * 2 * NP)
            hid = dot_nn(n2[block], w1[c]) + upb[:, span]
            back = dot_nt(gs[block], w2[span])
            phi = 0.5 * (1.0 + lax.erf(hid * (1.0 / math.sqrt(2.0))))
            density = jnp.exp(-0.5 * hid * hid) * (1.0 / math.sqrt(2.0 * math.pi))
            a = (hid * phi).astype(bf16)
            g = (back * (phi + hid * density)).astype(bf16)
            act[block] = a
            gh[block] = g
            bias_sum = bias_sum + jnp.sum(g.astype(f32), axis=0, keepdims=True)
            summed[block] += dot_nn(a, w2[span])
            gn2[block] += dot_nt(g, w1[c])
        bgrad[:, span] = bias_sum
        up_grad = dot_tn(n2[...], gh[...])
        down_grad = dot_tn(act[...], gs[...])
        for r in range(T):
            for cc in range(per):
                tiles[c, r * per + cc] = up_grad[
                    r * B : (r + 1) * B, cc * B : (cc + 1) * B
                ].astype(bf16)
        for r in range(per):
            for cc in range(T):
                tiles[c, T * per + r * T + cc] = down_grad[
                    r * B : (r + 1) * B, cc * B : (cc + 1) * B
                ].astype(bf16)

        @pl.loop(0, T * per)
        def _(t):
            r = t // per
            g = c * per + lax.rem(t, per)
            p = g // local
            b = r * local + lax.rem(g, local)
            pltpu.make_async_copy(
                tiles.at[c, t], tiles_out.at[place(own[b], p)], sem_out
            ).start()
            g2 = c * per + t // T
            p2 = g2 // local
            b2 = half + lax.rem(g2, local) * T + lax.rem(t, T)
            pltpu.make_async_copy(
                tiles.at[c, T * per + t], tiles_out.at[place(own[b2], p2)], sem_out
            ).start()

    s4 = jnp.zeros((1, D), f32)
    s5 = jnp.zeros((1, D), f32)
    s6 = jnp.zeros((1, D), f32)
    s7 = jnp.zeros((1, D), f32)
    s8 = jnp.zeros((1, D), f32)
    s9 = jnp.zeros((1, D), f32)
    for img in range(imgs):
        block = slice(img * NP, (img + 1) * NP)
        up = cot[img]
        middle = mid[img]
        sm = summed[block] + vec[8:9]
        out[img] = (middle + vec[9:10] * sm).astype(bf16)
        s9 += jnp.sum(up * sm, axis=0, keepdims=True)
        s8 += jnp.sum(gs[block].astype(f32), axis=0, keepdims=True)
        x, inv = norm_parts(middle)
        gn = gn2[block]
        s6 += jnp.sum(gn * x, axis=0, keepdims=True)
        s7 += jnp.sum(gn, axis=0, keepdims=True)
        gm = up + norm_back(gn, x, inv, vec[6:7])
        gmid[img] = gm
        gb = (vec[5:6] * gm).astype(bf16)
        gbra[img] = gb
        s4 += jnp.sum(gb.astype(f32), axis=0, keepdims=True)
        s5 += jnp.sum(gm * bra[img], axis=0, keepdims=True)
    sums[...] = jnp.concatenate([s4, s5, s6, s7, s8, s9, s9, s9], axis=0)
    pltpu.make_async_copy(tiles, tiles, sem_out).wait()


def feed_forward(mid, bra, n2, cot, slots, own, vec, up_bias, parts, each):
    imgs = mid.shape[0]
    rows = imgs * NP
    chunks = FF // CH
    per = CH // B
    return pl.pallas_call(
        partial(mlp_kernel, parts, each),
        in_specs=[SMEM, VMEM, VMEM, VMEM, VMEM, ANY, VMEM, VMEM],
        out_specs=[VMEM] * 5 + [ANY],
        out_shape=[
            shape((imgs, NP, D), bf16),
            shape((imgs, NP, D), f32),
            shape((imgs, NP, D), bf16),
            shape((8, D), f32),
            shape((1, FF), f32),
            shape(slots.shape, bf16),
        ],
        scratch_shapes=[
            pltpu.VMEM((chunks, D, CH), bf16),
            pltpu.VMEM((FF, D), bf16),
            pltpu.VMEM((rows, D), bf16),
            pltpu.VMEM((rows, CH), bf16),
            pltpu.VMEM((rows, CH), bf16),
            pltpu.VMEM((rows, D), f32),
            pltpu.VMEM((rows, D), f32),
            pltpu.VMEM((chunks, 2 * T * per, B, B), bf16),
            pltpu.SemaphoreType.DMA(()),
            pltpu.SemaphoreType.DMA(()),
        ],
        compiler_params=pltpu.CompilerParams(vmem_limit_bytes=LIMIT),
        name="feed_forward",
    )(own, mid, bra, n2.reshape(rows, D), cot, slots, vec, up_bias)


def backward_kernel(
    own,
    tok,
    w,
    q,
    k,
    v,
    att,
    lse,
    bias,
    gmid,
    gbra,
    vec,
    gin,
    grid,
    sums,
    tiles_out,
    n1,
    gatt,
    gqkv,
    tiles,
    sem,
):
    imgs = q.shape[0]
    for img in range(imgs):
        x, _ = norm_parts(tok[img].astype(f32))
        n1[img * NP : (img + 1) * NP] = (x * vec[0:1] + vec[1:2]).astype(bf16)
    for n in range(D // NL):
        lanes = slice(n * NL, (n + 1) * NL)
        got = dot_nt(gbra[...], w[3, lanes, :]).astype(bf16)
        for img in range(imgs):
            gatt[img, :, lanes] = got[img * NP : (img + 1) * NP]
    grid[...] = jnp.zeros_like(grid)

    @pl.loop(0, imgs)
    def _(img):
        side = lax.broadcasted_iota(jnp.int32, (1, B), 1) // HD
        here = pl.ds(pl.multiple_of(img * NP, 16), NP)
        for pair in range(H // 2):
            lanes = slice(pair * B, (pair + 1) * B)
            k_pair = k[img, :, lanes]
            v_pair = v[img, :, lanes]
            q_pair = pad_rows(q[img, :, lanes])
            g_pair = pad_rows(gatt[img, :, lanes])
            k_turn = k_pair.astype(f32).T.astype(bf16)
            gq = []
            gk = jnp.zeros((NP, B), f32)
            gv = jnp.zeros((NP, B), f32)
            for sub in range(2):
                h = pair * 2 + sub
                q_one = jnp.where(side == sub, q_pair, jnp.zeros_like(q_pair))
                g_one = jnp.where(side == sub, g_pair, jnp.zeros_like(g_pair))
                s = dot_nt(k_pair, q_one) + bias[h]
                p = jnp.exp(s - lse[img, h : h + 1])
                dp = dot_nt(v_pair, g_one)
                gv = gv + dot_nn(p.astype(bf16), g_one)
                inner = jnp.sum(p * dp, axis=0, keepdims=True)
                ds = (p * (dp - inner)).astype(bf16)
                gk = gk + dot_nn(ds, q_one)
                gq.append(dot_nn(k_turn[sub * HD : (sub + 1) * HD], ds))
                grid[h] += ds.astype(f32)
            turned = jnp.concatenate(gq, axis=0).T
            gqkv[here, lanes] = (turned[:NP] * HD**-0.5).astype(bf16)
            gqkv[here, D + pair * B : D + (pair + 1) * B] = gk.astype(bf16)
            gqkv[here, 2 * D + pair * B : 2 * D + (pair + 1) * B] = gv.astype(bf16)

    def put(m, n, grad):
        for r in range(T):
            for cc in range(NL // B):
                tiles[m * T * T + r * T + n * (NL // B) + cc] = grad[
                    r * B : (r + 1) * B, cc * B : (cc + 1) * B
                ].astype(bf16)

    for n in range(D // NL):
        lanes = slice(n * NL, (n + 1) * NL)
        put(3, n, dot_tn(att[...], gbra[:, lanes]))
    for m in range(3):
        for n in range(D // NL):
            put(m, n, dot_tn(n1[...], gqkv[:, m * D + n * NL : m * D + (n + 1) * NL]))

    @pl.loop(0, own.shape[0])
    def _(b):
        pltpu.make_async_copy(tiles.at[b], tiles_out.at[own[b]], sem).start()

    s0 = jnp.zeros((1, D), f32)
    s1 = jnp.zeros((1, D), f32)
    s2 = jnp.zeros((1, D), f32)
    s3 = jnp.zeros((1, D), f32)
    for img in range(imgs):
        here = slice(img * NP, (img + 1) * NP)
        gq = gqkv[here, 0:D]
        gk = gqkv[here, D : 2 * D]
        gv = gqkv[here, 2 * D : 3 * D]
        gn = dot_nt(gq, w[0]) + dot_nt(gk, w[1]) + dot_nt(gv, w[2])
        x, inv = norm_parts(tok[img].astype(f32))
        s0 += jnp.sum(gn * x, axis=0, keepdims=True)
        s1 += jnp.sum(gn, axis=0, keepdims=True)
        s2 += jnp.sum(gq.astype(f32), axis=0, keepdims=True)
        s3 += jnp.sum(gv.astype(f32), axis=0, keepdims=True)
        gin[img] = gmid[img] + norm_back(gn, x, inv, vec[0:1])
    sums[...] = jnp.concatenate([s0, s1, s2, s3, s3, s3, s3, s3], axis=0)
    pltpu.make_async_copy(tiles, tiles, sem).wait()


def backward_attention(tok, w, q, k, v, att, lse, bias, gmid, gbra, own, vec, slot_total):
    imgs = tok.shape[0]
    rows = imgs * NP
    return pl.pallas_call(
        backward_kernel,
        in_specs=[SMEM] + [VMEM] * 11,
        out_specs=[VMEM] * 3 + [ANY],
        out_shape=[
            shape((imgs, NP, D), f32),
            shape((H, NP, NL), f32),
            shape((8, D), f32),
            shape((slot_total, B, B), bf16),
        ],
        scratch_shapes=[
            pltpu.VMEM((rows, D), bf16),
            pltpu.VMEM((imgs, NP, D), bf16),
            pltpu.VMEM((rows, 3 * D), bf16),
            pltpu.VMEM((4 * T * T, B, B), bf16),
            pltpu.SemaphoreType.DMA(()),
        ],
        compiler_params=pltpu.CompilerParams(vmem_limit_bytes=LIMIT),
        name="backward_attention",
    )(
        own,
        tok,
        w,
        q,
        k,
        v,
        att.reshape(rows, D),
        lse,
        bias,
        gmid,
        gbra.reshape(rows, D),
        vec,
    )


NB = 16


def split_two(x):
    first = x.astype(bf16)
    return first, (x - first.astype(f32)).astype(bf16)


def wide_dot(x, y, dims):
    xa, xb = split_two(x)
    ya, yb = split_two(y)
    xs = jnp.concatenate([xa, xa, xb], axis=dims[0])
    ys = jnp.concatenate([ya, yb, ya], axis=dims[1])
    return lax.dot_general(
        xs, ys, (((dims[0],), (dims[1],)), ((), ())), preferred_element_type=f32
    )


def orth_turned(mats):
    count = len(mats)
    tails = []
    for a in mats:
        turned = a.T
        tails.append(jnp.concatenate([wide_dot(turned, turned, (1, 1)), turned], axis=1))
    rows = lax.broadcasted_iota(jnp.int32, (NB, 1), 0)
    eye = lax.broadcasted_iota(jnp.int32, (NB, NB), 0) == lax.broadcasted_iota(
        jnp.int32, (NB, NB), 1
    )
    outs = [[] for _ in range(count)]
    for p in range(B // NB):
        base = p * NB
        strips = [t[:NB] for t in tails]
        for kk in range(NB):
            at = base + kk
            for m in range(count):
                s = strips[m]
                pivot_row = jnp.broadcast_to(s[kk : kk + 1, :], (NB, 2 * B))
                factor = s[:, at : at + 1] * (1.0 / s[kk : kk + 1, at : at + 1])
                strips[m] = s - jnp.where(rows > kk, factor, 0.0) * pivot_row
        for m in range(count):
            s = strips[m]
            diag = jnp.sum(jnp.where(eye, s[:, base : base + NB], 0.0), axis=1, keepdims=True)
            u = s * lax.rsqrt(diag)
            outs[m].append(u[:, B:])
            if base + NB < B:
                tails[m] = tails[m][NB:] - wide_dot(u[:, base + NB : B], u, (0, 0))
    return [jnp.concatenate(o, axis=0) for o in outs]


def soap_kernel(live, grads, state, update, copy):
    count = grads.shape[0]
    mats = []
    first_slot = pl.program_id(0) * count
    gs = []
    for i in range(count):
        g = jnp.where(live[first_slot + i] > 0, grads[i].astype(f32), 0.0)
        gs.append(g)
        left = beta_stat * state[i, 3] + (1.0 - beta_stat) * wide_dot(g, g, (1, 1))
        right = beta_stat * state[i, 4] + (1.0 - beta_stat) * wide_dot(g, g, (0, 0))
        mats.append(wide_dot(left, state[i, 5], (1, 0)))
        mats.append(wide_dot(right, state[i, 6], (1, 0)))
    turned = orth_turned(mats)
    fix_one = 1.0 - beta_one**STEP
    fix_two = 1.0 - beta_two**STEP
    for i in range(count):
        tl, tr = turned[2 * i], turned[2 * i + 1]
        rotated = wide_dot(wide_dot(tl, gs[i], (1, 0)), tr, (1, 1))
        new_first = beta_one * state[i, 1] + (1.0 - beta_one) * rotated
        new_second = beta_two * state[i, 2] + (1.0 - beta_two) * rotated * rotated
        normalized = new_first / fix_one / (jnp.sqrt(new_second / fix_two) + adam_eps)
        step = wide_dot(wide_dot(tl, normalized, (0, 0)), tr, (1, 0))
        weight = state[i, 0]
        weight = weight - matrix_rate * (step + decay_rate * weight)
        update[i, 0] = weight
        update[i, 1] = new_first
        update[i, 2] = new_second
        update[i, 3] = tl.T
        update[i, 4] = tr.T
        copy[i] = weight.astype(bf16)


def soap_update(grads, state, live):
    slots = grads.shape[0]
    count = max(c for c in range(1, 10) if slots % c == 0)
    return pl.pallas_call(
        soap_kernel,
        grid_spec=pltpu.PrefetchScalarGridSpec(
            num_scalar_prefetch=1,
            grid=(slots // count,),
            in_specs=[
                pl.BlockSpec((count, B, B), lambda i, s: (i, 0, 0)),
                pl.BlockSpec((count, 7, B, B), lambda i, s: (i, 0, 0, 0)),
            ],
            out_specs=[
                pl.BlockSpec((count, 5, B, B), lambda i, s: (i, 0, 0, 0)),
                pl.BlockSpec((count, B, B), lambda i, s: (i, 0, 0)),
            ],
        ),
        out_shape=[shape((slots, 5, B, B), f32), shape((slots, B, B), bf16)],
        compiler_params=pltpu.CompilerParams(vmem_limit_bytes=LIMIT),
        name="soap",
    )(live, grads, state)


def adam_vector(grads, param, moments, step_number):
    new_first = beta_one * moments[0] + (1.0 - beta_one) * grads
    new_second = beta_two * moments[1] + (1.0 - beta_two) * grads * grads
    fix_one = 1.0 - beta_one**step_number
    fix_two = 1.0 - beta_two**step_number
    new_param = param - vector_rate * (new_first / fix_one) / (
        jnp.sqrt(new_second / fix_two) + adam_eps
    )
    return jnp.stack([grads, new_param, new_first, new_second])


def body(
    tokens,
    cotangent,
    rel_index,
    attn_owner,
    mlp_owner,
    attn_state,
    mlp_state,
    vec_param,
    vec_moments,
    rel_table,
    rel_table_moments,
    up_bias,
    up_bias_moments,
):
    both = ("dp", "mp")
    parts = lax.axis_size("mp")
    rank = lax.axis_index("dp") * parts + lax.axis_index("mp")
    imgs = tokens.shape[1] // NPOS
    attn_local = attn_state.shape[0]
    mlp_local = mlp_state.shape[1]
    attn_total = attn_local * lax.axis_size("dp") * parts

    attn_slots = lax.all_gather(attn_state[:, 0].astype(bf16), both, axis=0, tiled=True)
    mlp_slots = lax.all_gather(mlp_state[0, :, 0].astype(bf16), both, axis=0, tiled=True)

    wide_total = -(-rel_table.shape[1] // B) * B
    idx_t = jnp.pad(rel_index.T, ((0, NP - NPOS), (0, NL - NPOS)))
    table_pad = jnp.pad(rel_table, ((0, 0), (0, wide_total - rel_table.shape[1])))
    bias = table_lookup(idx_t, table_pad)

    def padded(x):
        return jnp.pad(x.reshape(imgs, NPOS, D), ((0, 0), (0, NP - NPOS), (0, 0)))

    def unpadded(x):
        return x[:, :NPOS].reshape(1, imgs * NPOS, D)

    tok = padded(tokens)
    cot = padded(cotangent)
    w, q, k, v, att, lse, mid, bra, n2 = forward_attention(
        tok, attn_slots, attn_owner, vec_param, bias
    )
    out, gmid, gbra, mlp_sums, bias_grad, mlp_grads = feed_forward(
        mid, bra, n2, cot, mlp_slots, mlp_owner, vec_param, up_bias[None], parts, mlp_local
    )
    mlp_mine = lax.psum_scatter(mlp_grads, both, scatter_dimension=0, tiled=True)
    gin, grid, attn_sums, attn_grads = backward_attention(
        tok, w, q, k, v, att, lse, bias, gmid, gbra, attn_owner, vec_param, attn_total
    )
    attn_mine = lax.psum_scatter(attn_grads, both, scatter_dimension=0, tiled=True)
    table_grad = table_accumulate(grid, idx_t, wide_total // B)
    table_grad = table_grad.transpose(1, 0, 2).reshape(16, wide_total)[:H, : rel_table.shape[1]]

    vector_grad = jnp.concatenate([attn_sums[:4], mlp_sums[:6]], axis=0)
    vector_total, table_total, bias_total = lax.psum(
        (vector_grad, table_grad, bias_grad[0]), both
    )

    def live(owner, first, count):
        mine = first + jnp.arange(count, dtype=jnp.int32)
        return jnp.any(owner[None, :] == mine[:, None], axis=1).astype(jnp.int32)

    mlp_result, mlp_copy = soap_update(
        mlp_mine,
        mlp_state[0],
        live(mlp_owner, lax.axis_index("dp") * mlp_local, mlp_local),
    )
    attn_result, attn_copy = soap_update(
        attn_mine, attn_state, live(attn_owner, rank * attn_local, attn_local)
    )
    return (
        unpadded(out),
        unpadded(gin),
        attn_result,
        attn_copy,
        mlp_result[None],
        mlp_copy[None],
        adam_vector(vector_total, vec_param, vec_moments, STEP),
        adam_vector(table_total, rel_table, rel_table_moments, STEP),
        adam_vector(bias_total, up_bias, up_bias_moments, STEP),
    )


def solution(mesh):
    placed = (
        P(("dp", "mp"), None, None),
        P(("dp", "mp"), None, None),
        P(),
        P(),
        P(),
        P(("dp", "mp"), None, None, None),
        P("mp", "dp", None, None, None),
        P(),
        P(),
        P(),
        P(),
        P(),
        P(),
    )
    return jax.shard_map(
        body,
        mesh=mesh,
        in_specs=placed,
        out_specs=(
            P(("dp", "mp"), None, None),
            P(("dp", "mp"), None, None),
            P(("dp", "mp"), None, None, None),
            P(("dp", "mp"), None, None),
            P("mp", "dp", None, None, None),
            P("mp", "dp", None, None),
            P(),
            P(),
            P(),
        ),
        check_vma=False,
    )
```

time: 1900 us -> 746 us (0.39)
  other arithmetic: 672 us -> 15.3 us
  local copies, waits for them, and re-layouts: 567 us -> 25.8 us
  matrix products: 442 us -> 0 us
  waiting for transfers between devices: 119 us -> 463 us
  Pallas kernels: 0 us -> 221 us
  blocking collectives: 59 us -> 0 us
    another operation x19 -> x0, other arithmetic: 610 us -> none  [the longest x10 333 us: cholesky_orth(): factor = jnp.linalg.cholesky(gram)]
    dot_general x190 -> x0, matrix products: 438 us -> none  [the longest x25 74.4 us: one_group(): return jnp.dot(rel_table, onehot.T, precision=precise)]
    pallas_call x0 -> x7, Pallas kernels: none -> 221 us  [the longest x2 57.3 us: soap_update(): pl.pallas_call(soap_kernel, grid_spec=pltpu.PrefetchScalarGridSpec(num_sc...]
    gather x74 -> x0, local copies, waits for them, and re-layouts: 178 us -> none  [the longest x72 157 us: head_scores(): bias_head = bias_grid[position][:, position]]
    reduce_scatter x2, waiting for transfers between devices: 104 us -> 253 us  [the longest x1 139 us: body(): lax.psum_scatter(attn_grads, both, scatter_dimension=0, tiled=True)]
    psum x1, waiting for transfers between devices: 0.01 us -> 109 us  [body(): lax.psum((vector_grad, table_grad, bias_grad[0]), both)]
    all_gather x4 -> x2, waiting for transfers between devices: 15.2 us -> 99.5 us  [the longest x1 57.2 us: body(): lax.all_gather(mlp_state[0, :, 0].astype(bf16), both, axis=0, tiled=True)]
    dynamic_slice x88 -> x0, local copies, waits for them, and re-layouts: 59.6 us -> none  [the longest x25 28.6 us: table_accumulate(): lax.scan(one_group, jnp.zeros((head_count, rel_total), jnp.float32), (gro...]
  transfers between devices with their start and end apart: 9 -> 5, of which waited for: 2 -> 5; matrix products, arithmetic and copies ran while one was open for 50% -> 5% of each run, Pallas kernels for 0% -> 8%
where the time goes in v1:
time: 746 us; the launch traced here: 739 us
  waiting for transfers between devices  463 us (62%)
  Pallas kernels  221 us (30%)
  local copies, waits for them, and re-layouts  25.8 us (3%)
  other arithmetic  15.3 us (2%)
  between operations  14.2 us (2%)
    reduce_scatter x1, waiting for transfers between devices, body(): lax.psum_scatter(attn_grads, both, scatter_dimension=0, tiled=True)  139 us
    reduce_scatter x1, waiting for transfers between devices, body(): lax.psum_scatter(mlp_grads, both, scatter_dimension=0, tiled=True)  113 us
    psum x1, waiting for transfers between devices, body(): lax.psum((vector_grad, table_grad, bias_grad[0]), both)  109 us
    pallas_call x2, Pallas kernels, soap_update(): pl.pallas_call(soap_kernel, grid_spec=pltpu.PrefetchScalarGridSpec(num_sc...  57.3 us
    all_gather x1, waiting for transfers between devices, body(): lax.all_gather(mlp_state[0, :, 0].astype(bf16), both, axis=0, tiled=True)  57.2 us
    pallas_call x1, Pallas kernels, feed_forward(): pl.pallas_call(partial(mlp_kernel, parts, each), in_specs=[SMEM, VMEM, VM...  51.5 us
    all_gather x1, waiting for transfers between devices, body(): lax.all_gather(attn_state[:, 0].astype(bf16), both, axis=0, tiled=True)  42.2 us
    pallas_call x1, Pallas kernels, table_accumulate(): pl.pallas_call(accumulate_kernel, in_specs=[VMEM, VMEM], out_specs=VMEM,...  38.8 us
  transfers between devices with their start and end apart: 5, of which 5 were waited for; matrix products, arithmetic and copies ran while one was open for 5% of the time, Pallas kernels for 8%

profile of v1, /device:TPU:0, one launch (start us, length us, event | category | flops | bytes accessed | tf_op | source)
XLA Modules:
  0.0 739.3 jit_solution(9985597064398544800)
XLA Ops:
  7.2 1.8 slice.62
  9.1 0.0 all-gather.7.cloned.1.call-start
  9.1 1.8 slice.61
  11.0 0.0 all-reduce.7.cloned.1.call-start
  11.0 1.0 copy.55
  12.1 2.6 reshape.66
  14.7 7.8 %reduce = f32[788,768]{1,0:T(8,128)} reduce(f32[1,788,768]{2,0,1:T(1,128)S(1)} %copy-done.1, f32[]{:T(128)} %constant.74), dimensions={0}, to_apply=%param.14.reduce_sub_computation | reduce | bytes 4841476 | tf_op args[1]
  22.5 2.0 reshape.68
  24.5 0.6 pad.18.table_ref
  25.2 1.7 pad.19.cot
  26.9 0.7 pad.17.idx_ref
  27.6 8.6 %table_lookup.1.bias = f32[12,208,256]{2,1,0:T(8,128)} custom-call(s32[208,256]{1,0:T(8,128)} %pad.17.idx_ref, f32[12,768]{1,0:T(8,128)} %pad.18.table_ref), custom_call_target="tpu_custom_call" | custom-call | tf_op jit(solution)/shard_map/table_lookup/pallas_call | solution.py:95
  36.2 1.1 pad.16.tok
  37.3 42.2 %all-gather.5.cloned.1.call-done = bf16[160,1,128,128]{3,2,1,0:T(8,128)(2,1)} async-done(((bf16[5,1,128,128]{3,2,1,0:T(8,128)(2,1)}), bf16[160,1,128,128]{3,2,1,0:T(8,128)(2,1)}) %all-gather.5.cloned.1.call-update) | async-done | bytes 5242896 | tf_op jit(solution)/shard_map/all_gather | solution.py:701
  79.6 27.2 %forward_attention.1 = (bf16[4,768,768]{2,1,0:T(8,128)(2,1)}, bf16[4,208,768]{2,1,0:T(8,128)(2,1)}, bf16[4,208,768]{2,1,0:T(8,128)(2,1)}, bf16[4,208,768]{2,1,0:...) custom-call(s32[144]{0:T(256)} %own.5, ...), custom_call_target="tpu_custom_call" | custom-call | tf_op jit(solution)/shard_map/forward_attention/pallas_call | solution.py:219
  106.8 57.2 %all-gather.7.cloned.1.call-done = bf16[1,288,1,128,128]{4,3,2,0,1:T(8,128)(2,1)} async-done(((bf16[1,9,1,128,128]{4,3,2,0,1:T(8,128)(2,1)}), bf16[1,288,1,128,128]{4,3,2,0,1:T(8,128)(2,1)}) %all-gather.7.cloned.1.call-update) | async-done | bytes 9437200 | tf_op jit(solution)/shard_map/all_gather | solution.py:702
  164.0 51.5 %feed_forward.1 = (bf16[4,208,768]{2,1,0:T(8,128)(2,1)}, f32[4,208,768]{2,1,0:T(8,128)}, bf16[4,208,768]{2,1,0:T(8,128)(2,1)}, f32[8,768]{1,0:T(8,128)}, f32[1,3...) custom-call(s32[144]{0:T(256)} %own.4, f32[4,208,768]{2,1,0:T(8,128)} %get-tuple-element.32.mid, ...), custom_call_target="tpu_custom_call" | custom-call | tf_op jit(solution)/shard_map/feed_forward/pallas_call | solution.py:392
  215.6 37.9 %backward_attention.1 = (f32[4,208,768]{2,1,0:T(8,128)}, f32[12,208,256]{2,1,0:T(8,128)}, f32[8,768]{1,0:T(8,128)}, bf16[160,128,128]{2,1,0:T(8,128)(2,1)}) custom-call(s32[144]{0:T(256)} %own.5, bf16[4,208,768]{2,1,0:T(8,128)(2,1)} %pad.16.tok, bf16[4,768,768]{2,1,0:T(8,128)(2,1)} %get-tuple-element.36.w, bf16[4,208,768]{2,1,0:T(8,128)(2,1)} %get-tuple-element.37.q, ...), custom_call_target="tpu_custom_call" | custom-call | tf_op jit(solution)/shard_map/backward_attention/pallas_call | solution.py:528
  253.4 0.7 slice.45
  254.2 38.8 %table_accumulate.1 = f32[6,16,128]{2,1,0:T(8,128)} custom-call(f32[12,208,256]{2,1,0:T(8,128)} %get-tuple-element.53.grid_ref, s32[208,256]{1,0:T(8,128)} %pad.17.idx_ref), custom_call_target="tpu_custom_call" | custom-call | tf_op jit(solution)/shard_map/table_accumulate/pallas_call | solution.py:134
  293.0 1.4 copy_bitcast_fusion
  294.5 0.6 pad_maximum_fusion.2
  295.1 0.0 reduce-scatter.3.cloned.1.call-start
  295.2 0.5 reduce-scatter.3.cloned.1.call-update
  295.8 0.5 reduce-scatter.5.cloned.1.call-update
  296.3 0.1 copy-done.9
  296.4 0.2 compare_reduce_fusion.1
  296.6 0.5 convert_element_type.22.live
  297.1 0.2 compare_reduce_fusion
  297.3 0.5 convert_element_type.23.live
  297.9 0.1 fusion.14
  298.0 1.9 slice.44
  299.9 3.7 reshape.76
  303.7 1.4 slice.43
  305.1 1.3 reshape.69
  306.4 109.2 %all-reduce.7.cloned.1.call-done = (f32[10,768]{1,0:T(8,128)}, f32[12,732]{1,0:T(8,128)}, f32[3072]{0:T(1024)}) async-done(((f32[10,768]{1,0:T(8,128)}, f32[12,732]{1,0:T(8,128)}, f32[3072]{0:T(1024)}), (f32[10,768]{1,0:T(8,128)}, f32[12,732]{1,0:T(8,128)}, f32[3072]{0:T(1024)})) %all-reduce.7.cloned.1.call-update) | async-done | bytes 78160 | tf_op jit(solution)/shard_map/psum | solution.py:732
  415.6 0.8 subtract_bitcast_fusion
  416.4 0.8 pad_maximum_fusion.1
  417.2 0.8 copy.64
  418.0 0.8 subtract_bitcast_fusion.1
  418.8 0.8 pad_maximum_fusion
  419.7 0.7 copy.63
  420.4 0.7 divide_subtract_fusion
  421.1 1.4 pad_maximum_fusion.3
  422.5 139.5 %reduce-scatter.3.cloned.1.call-done.grads = bf16[5,128,128]{2,1,0:T(8,128)(2,1)} async-done(((bf16[160,128,128]{2,1,0:T(8,128)(2,1)}), bf16[5,128,128]{2,1,0:T(8,128)(2,1)}) %reduce-scatter.3.cloned.1.call-update) | async-done | bytes 163856 | tf_op jit(solution)/shard_map/reduce_scatter | solution.py:727
  562.0 25.4 %soap.2 = (f32[5,5,128,128]{3,2,1,0:T(8,128)}, bf16[5,128,128]{2,1,0:T(8,128)(2,1)}) custom-call(s32[5]{0:T(128)} %convert_element_type.22.live, bf16[5,128,128]{2,1,0:T(8,128)(2,1)} %reduce-scatter.3.cloned.1.call-done.grads, f32[5,7,128,128]{3,2,1,0:T(8,128)} %state.1), custom_call_target="tpu_custom_call" | custom-call | tf_op jit(solution)/shard_map/soap/pallas_call | solution.py:647
  587.4 113.3 %reduce-scatter.5.cloned.1.call-done.grads = bf16[9,128,128]{2,1,0:T(8,128)(2,1)} async-done(((bf16[288,128,128]{2,1,0:T(8,128)(2,1)}), bf16[9,128,128]{2,1,0:T(8,128)(2,1)}) %reduce-scatter.5.cloned.1.call-update) | async-done | bytes 294928 | tf_op jit(solution)/shard_map/reduce_scatter | solution.py:723
  700.7 31.9 %soap.3 = (f32[9,5,128,128]{3,2,1,0:T(8,128)}, bf16[9,128,128]{2,1,0:T(8,128)(2,1)}) custom-call(s32[9]{0:T(128)} %convert_element_type.23.live, bf16[9,128,128]{2,1,0:T(8,128)(2,1)} %reduce-scatter.5.cloned.1.call-done.grads, f32[9,7,128,128]{3,2,1,0:T(8,128)} %bitcast.75), custom_call_target="tpu_custom_call" | custom-call | tf_op jit(solution)/shard_map/soap/pallas_call | solution.py:647
  (30 shorter events, 0.3 us)
Async XLA Ops:
  7.2 7.5 %copy-start.1 = (f32[1,788,768]{2,0,1:T(1,128)S(1)}, f32[1,788,768]{2,0,1:T(1,128)}, u32[]{:S(2)}) copy-start(f32[1,788,768]{2,0,1:T(1,128)} %param.14) | copy-start | bytes 7262212
  7.2 72.4 %all-gather.5.cloned.1.call-start = ((), (), s32[]{:S(2)}) async-start(), calls=%async_computation.4 | async-start | bytes 5406720 | tf_op jit(solution)/shard_map/all_gather | solution.py:701
  9.1 155.0 %all-gather.7.cloned.1.call-start = ((), (), s32[]{:S(2)}) async-start(), calls=%async_computation.5 | async-start | bytes 9732096 | tf_op jit(solution)/shard_map/all_gather | solution.py:702
  11.0 404.6 %all-reduce.7.cloned.1.call-start = ((), (), s32[]{:S(2)}) async-start(), calls=%async_computation.6 | async-start | bytes 221184 | tf_op jit(solution)/shard_map/psum | solution.py:732
  22.5 2.0 copy-start.3
  26.9 9.3 %copy-start = (bf16[4,197,768]{2,1,0:T(8,128)(2,1)S(1)}, bf16[4,197,768]{2,1,0:T(8,128)(2,1)}, u32[]{:S(2)}) copy-start(bf16[4,197,768]{2,1,0:T(8,128)(2,1)} %reshape.66) | copy-start | bytes 3631108
  253.4 41.0 %copy-start.8 = (f32[8,768]{1,0:T(8,128)S(1)}, f32[8,768]{1,0:T(8,128)}, u32[]{:S(2)}) copy-start(f32[8,768]{1,0:T(8,128)} %get-tuple-element.52) | copy-start | bytes 73732
  295.1 266.9 %reduce-scatter.3.cloned.1.call-start = ((), (), s32[]{:S(2)}) async-start(), calls=%async_computation.2 | async-start | bytes 5406720 | tf_op jit(solution)/shard_map/reduce_scatter | solution.py:727
  295.7 405.0 %reduce-scatter.5.cloned.1.call-start = ((), (), s32[]{:S(2)}) async-start(), calls=%async_computation.3 | async-start | bytes 9732096 | tf_op jit(solution)/shard_map/reduce_scatter | solution.py:723
  295.7 0.7 copy-start.9
  295.8 1.4 copy-start.10
  295.8 2.1 copy-start.5
  295.8 2.1 copy-start.4
  295.8 2.2 copy-start.7
  303.6 114.4 %copy-start.2 = (f32[10,768]{1,0:T(8,128)S(1)}, f32[10,768]{1,0:T(8,128)}, u32[]{:S(2)}) copy-start(f32[10,768]{1,0:T(8,128)} %vec.5) | copy-start | bytes 92164
  305.0 115.3 %copy-start.6 = (f32[3072]{0:T(1024)S(1)}, f32[3072]{0:T(1024)}, u32[]{:S(2)}) copy-start(f32[3072]{0:T(1024)} %param.24) | copy-start | bytes 36868
Sparse Core Ops, SparseCore 0:
  11.4 68.0 all-gather.4
  83.0 80.9 all-gather.6
  295.2 120.2 all-reduce.6
  417.7 144.2 reduce-scatter.2
  567.7 132.9 reduce-scatter.4

commit v2 on v1

--- a/solution.py
+++ b/solution.py
@@ -66,6 +66,337 @@
         - jnp.mean(tangent, axis=-1, keepdims=True)
         - scaled * jnp.mean(tangent * scaled, axis=-1, keepdims=True)
     )
+
+
+MESH = pl.DeviceIdType.MESH
+COPIES = 35
+
+
+def own_kernels(dp_total, parts):
+    return dp_total == 16 and parts == 2
+
+
+class Place:
+    def __init__(self):
+        dp = lax.axis_index("dp")
+        self.y = lax.axis_index("mp")
+        self.z = dp // 4
+        self.x = lax.rem(dp // 2, 2)
+        self.c = lax.rem(dp, 2)
+
+    def rank(self, d=0, dx=0, dc=0, dy=0):
+        z = lax.rem(self.z + d + 4, 4)
+        x = 1 - self.x if dx else self.x
+        c = 1 - self.c if dc else self.c
+        y = 1 - self.y if dy else self.y
+        return ((z * 2 + x) * 2 + c) * 2 + y
+
+    def device(self, d=0, dx=0, dc=0, dy=0):
+        z = lax.rem(self.z + d + 4, 4)
+        x = 1 - self.x if dx else self.x
+        c = 1 - self.c if dc else self.c
+        y = 1 - self.y if dy else self.y
+        return ((z * 2 + x) * 2 + c, y)
+
+    def greet(self):
+        barrier = pltpu.get_barrier_semaphore()
+        for d, dx, dc, dy in PARTNERS:
+            pl.semaphore_signal(
+                barrier, inc=1, device_id=self.device(d, dx, dc, dy), device_id_type=MESH
+            )
+        pl.semaphore_wait(barrier, len(PARTNERS))
+
+
+PARTNERS = ((1, 0, 0, 0), (2, 0, 0, 0), (3, 0, 0, 0), (0, 1, 0, 0), (0, 0, 1, 0), (0, 0, 0, 1))
+
+
+class Copies:
+    def __init__(self, place, send, recv):
+        self.place = place
+        self.send = send
+        self.recv = recv
+        self.made = {}
+
+    def start(self, key, src, dst, **to):
+        i = len(self.made)
+        copy = pltpu.make_async_remote_copy(
+            src_ref=src,
+            dst_ref=dst,
+            send_sem=self.send.at[i],
+            recv_sem=self.recv.at[i],
+            device_id=self.place.device(**to),
+            device_id_type=MESH,
+        )
+        copy.start()
+        self.made[key] = copy
+
+    def arrived(self, key):
+        self.made[key].wait_recv()
+
+    def sent(self):
+        for copy in self.made.values():
+            copy.wait_send()
+
+
+class Gather(Copies):
+    def __init__(self, place, own, full, n, send, recv, local):
+        super().__init__(place, send, recv)
+        self.own = own
+        self.full = full
+        self.n = n
+        self.half = n // 2
+        self.local = pltpu.make_async_copy(own, self.at(), local)
+
+    def at(self, d=0, dx=0, dc=0, dy=0, lo=0, hi=None):
+        hi = self.n if hi is None else hi
+        return self.full.at[pl.ds(self.place.rank(d, dx, dc, dy) * self.n + lo, hi - lo)]
+
+    def spread(self, d):
+        src = self.own if d == 0 else self.at(d=-d)
+        dst = self.at(d=-d)
+        self.start(("x", d), src, dst, dx=1)
+        self.start(("y", d), src, dst, dy=1)
+        self.start(("c", d, 0, 0), src, dst, dc=1)
+
+    def along(self, d):
+        self.start(("z", d), self.own, self.at(), d=d)
+
+    def share(self, d, dx, dy):
+        ref = self.at(d=-d, dx=dx, dy=dy)
+        self.start(("c", d, dx, dy), ref, ref, dc=1)
+
+    def corner(self, d):
+        ref = self.at(d=-d, dy=1, lo=self.half)
+        self.start(("xd", d), ref, ref, dx=1)
+        ref = self.at(d=-d, dx=1, hi=self.half)
+        self.start(("yd", d), ref, ref, dy=1)
+
+    def sides(self, d):
+        self.arrived(("x", d))
+        self.share(d, 1, 0)
+        self.arrived(("y", d))
+        self.share(d, 0, 1)
+
+    def cornered(self, d):
+        self.arrived(("xd", d))
+        self.arrived(("yd", d))
+        self.share(d, 1, 1)
+
+    def step(self, i):
+        if i == 0:
+            self.local.start()
+            self.along(1)
+            self.spread(0)
+        elif i == 1:
+            self.arrived(("z", 1))
+            self.along(3)
+            self.spread(1)
+            self.sides(0)
+        elif i == 2:
+            self.arrived(("z", 3))
+            self.along(2)
+            self.spread(3)
+            self.sides(1)
+            self.corner(0)
+        elif i == 3:
+            self.corner(1)
+            self.sides(3)
+        elif i == 4:
+            self.arrived(("z", 2))
+            self.spread(2)
+            self.cornered(0)
+            self.corner(3)
+            self.cornered(1)
+        elif i == 5:
+            self.sides(2)
+            self.corner(2)
+            self.cornered(3)
+        else:
+            self.cornered(2)
+            for d in range(4):
+                for dx in range(2):
+                    for dy in range(2):
+                        self.arrived(("c", d, dx, dy))
+            self.local.wait()
+            self.sent()
+
+
+GATHER_STEPS = 7
+
+
+class Scatter(Copies):
+    def __init__(self, place, full, n, acc, peer, side, corner, along, send, recv):
+        super().__init__(place, send, recv)
+        self.full = full
+        self.n = n
+        self.half = n // 2
+        self.acc = acc
+        self.peer = peer
+        self.side = side
+        self.cor = corner
+        self.col = along
+
+    def block(self, d, dx, dc, dy):
+        return pl.ds(self.place.rank(d, dx, dc, dy) * self.n, self.n)
+
+    def core(self, d):
+        for dx in range(2):
+            for dy in range(2):
+                self.start(
+                    ("c", d, dx, dy),
+                    self.full.at[self.block(d, dx, 1, dy)],
+                    self.peer.at[d, dx, dy],
+                    dc=1,
+                )
+
+    def pair(self, d, dx, dy):
+        self.arrived(("c", d, dx, dy))
+        n = self.n
+
+        @pl.loop(0, n)
+        def _(i):
+            mine = self.full[self.place.rank(d, dx, 0, dy) * n + i].astype(f32)
+            self.acc[d, dx, dy, i] = (mine + self.peer[d, dx, dy, i].astype(f32)).astype(bf16)
+
+    def add(self, d, dx, dy, other, lo, hi):
+        @pl.loop(lo, hi)
+        def _(i):
+            total = self.acc[d, dx, dy, i].astype(f32) + other[i - lo].astype(f32)
+            self.acc[d, dx, dy, i] = total.astype(bf16)
+
+    def corner(self, d):
+        self.pair(d, 1, 1)
+        h, n = self.half, self.n
+        self.start(("xd", d), self.acc.at[d, 1, 1, pl.ds(0, h)], self.cor.at[d, pl.ds(0, h)], dx=1)
+        self.start(
+            ("yd", d), self.acc.at[d, 1, 1, pl.ds(h, n - h)], self.cor.at[d, pl.ds(h, n - h)], dy=1
+        )
+        self.pair(d, 1, 0)
+        self.pair(d, 0, 1)
+        self.pair(d, 0, 0)
+
+    def sides(self, d):
+        h, n = self.half, self.n
+        self.arrived(("yd", d))
+        self.add(d, 1, 0, self.cor.at[d, pl.ds(h, n - h)], h, n)
+        self.start(("x", d), self.acc.at[d, 1, 0], self.side.at[d, 0], dx=1)
+        self.arrived(("xd", d))
+        self.add(d, 0, 1, self.cor.at[d, pl.ds(0, h)], 0, h)
+        self.start(("y", d), self.acc.at[d, 0, 1], self.side.at[d, 1], dy=1)
+
+    def along(self, d):
+        self.arrived(("x", d))
+        self.arrived(("y", d))
+
+        @pl.loop(0, self.n)
+        def _(i):
+            total = (
+                self.acc[d, 0, 0, i].astype(f32)
+                + self.side[d, 0, i].astype(f32)
+                + self.side[d, 1, i].astype(f32)
+            )
+            self.acc[d, 0, 0, i] = total.astype(bf16)
+
+        if d > 0:
+            self.start(("z", d), self.acc.at[d, 0, 0], self.col.at[d - 1], d=d)
+
+    def step(self, i, out=None):
+        if i == 0:
+            for d in (2, 3, 0, 1):
+                self.core(d)
+            self.corner(2)
+            self.corner(3)
+        elif i == 1:
+            self.sides(2)
+            self.corner(0)
+        elif i == 2:
+            self.along(2)
+            self.corner(1)
+            self.sides(3)
+        elif i == 3:
+            self.along(3)
+            self.sides(1)
+        elif i == 4:
+            self.along(1)
+            self.sides(0)
+        else:
+            self.along(0)
+            for d in (1, 2, 3):
+                self.arrived(("z", d))
+
+            @pl.loop(0, self.n)
+            def _(i):
+                out[i] = (
+                    (self.acc[0, 0, 0, i].astype(f32) + self.col[0, i].astype(f32))
+                    + self.col[1, i].astype(f32)
+                ) + self.col[2, i].astype(f32)
+
+            self.sent()
+
+
+SCATTER_STEPS = 6
+
+
+def scatter_scratch(n):
+    return [
+        pltpu.VMEM((4, 2, 2, n, B, B), bf16),
+        pltpu.VMEM((4, 2, 2, n, B, B), bf16),
+        pltpu.VMEM((4, 2, n, B, B), bf16),
+        pltpu.VMEM((4, n, B, B), bf16),
+        pltpu.VMEM((3, n, B, B), bf16),
+        pltpu.SemaphoreType.DMA((COPIES,)),
+        pltpu.SemaphoreType.DMA((COPIES,)),
+    ]
+
+
+def gather_kernel(n, own, full, send, recv, local):
+    place = Place()
+    place.greet()
+    moves = Gather(place, own, full, n, send, recv, local)
+    for i in range(GATHER_STEPS):
+        moves.step(i)
+
+
+def gather_blocks(own, cid):
+    n = own.shape[0]
+    return pl.pallas_call(
+        partial(gather_kernel, n),
+        in_specs=[VMEM],
+        out_specs=VMEM,
+        out_shape=shape((32 * n, B, B), bf16),
+        scratch_shapes=[
+            pltpu.SemaphoreType.DMA((COPIES,)),
+            pltpu.SemaphoreType.DMA((COPIES,)),
+            pltpu.SemaphoreType.DMA(()),
+        ],
+        compiler_params=pltpu.CompilerParams(
+            collective_id=cid, has_side_effects=True, vmem_limit_bytes=LIMIT
+        ),
+        name=f"gather{cid}",
+    )(own)
+
+
+def scatter_kernel(n, full, out, acc, peer, side, corner, along, send, recv):
+    place = Place()
+    place.greet()
+    moves = Scatter(place, full, n, acc, peer, side, corner, along, send, recv)
+    for i in range(SCATTER_STEPS):
+        moves.step(i, out)
+
+
+def scatter_blocks(full, cid):
+    n = full.shape[0] // 32
+    return pl.pallas_call(
+        partial(scatter_kernel, n),
+        in_specs=[VMEM],
+        out_specs=VMEM,
+        out_shape=shape((n, B, B), f32),
+        scratch_shapes=scatter_scratch(n),
+        compiler_params=pltpu.CompilerParams(
+            collective_id=cid, has_side_effects=True, vmem_limit_bytes=LIMIT
+        ),
+        name=f"scatter{cid}",
+    )(full)
 
 
 def lookup_kernel(idx_ref, table_ref, out_ref, spread):
@@ -698,8 +1029,20 @@
     mlp_local = mlp_state.shape[1]
     attn_total = attn_local * lax.axis_size("dp") * parts
 
-    attn_slots = lax.all_gather(attn_state[:, 0].astype(bf16), both, axis=0, tiled=True)
-    mlp_slots = lax.all_gather(mlp_state[0, :, 0].astype(bf16), both, axis=0, tiled=True)
+    mine = own_kernels(lax.axis_size("dp"), parts)
+
+    def gathered(own, cid):
+        if mine:
+            return gather_blocks(own, cid)
+        return lax.all_gather(own, both, axis=0, tiled=True)
+
+    def scattered(full, cid):
+        if mine:
+            return scatter_blocks(full, cid)
+        return lax.psum_scatter(full, both, scatter_dimension=0, tiled=True)
+
+    attn_slots = gathered(attn_state[:, 0].astype(bf16), 0)
+    mlp_slots = gathered(mlp_state[0, :, 0].astype(bf16), 1)
 
     wide_total = -(-rel_table.shape[1] // B) * B
     idx_t = jnp.pad(rel_index.T, ((0, NP - NPOS), (0, NL - NPOS)))
@@ -720,11 +1063,11 @@
     out, gmid, gbra, mlp_sums, bias_grad, mlp_grads = feed_forward(
         mid, bra, n2, cot, mlp_slots, mlp_owner, vec_param, up_bias[None], parts, mlp_local
     )
-    mlp_mine = lax.psum_scatter(mlp_grads, both, scatter_dimension=0, tiled=True)
+    mlp_mine = scattered(mlp_grads, 2)
     gin, grid, attn_sums, attn_grads = backward_attention(
         tok, w, q, k, v, att, lse, bias, gmid, gbra, attn_owner, vec_param, attn_total
     )
-    attn_mine = lax.psum_scatter(attn_grads, both, scatter_dimension=0, tiled=True)
+    attn_mine = scattered(attn_grads, 3)
     table_grad = table_accumulate(grid, idx_t, wide_total // B)
     table_grad = table_grad.transpose(1, 0, 2).reshape(16, wide_total)[:H, : rel_table.shape[1]]
 

time: 746 us -> 472 us (0.63)
  waiting for transfers between devices: 463 us -> 0.02 us
  Pallas kernels: 221 us -> 413 us
    reduce_scatter x2 -> x0, waiting for transfers between devices: 253 us -> none  [the longest x1 139 us: body(): lax.psum_scatter(attn_grads, both, scatter_dimension=0, tiled=True)]
    pallas_call x0 -> x4, Pallas kernels: none -> 181 us  [the longest x2 91.2 us: scatter_blocks(): pl.pallas_call(partial(scatter_kernel, n), in_specs=[VMEM], out_specs=VME...]
    psum x1, waiting for transfers between devices: 109 us -> 0.01 us  [body(): lax.psum((vector_grad, table_grad, bias_grad[0]), both)]
    all_gather x2 -> x0, waiting for transfers between devices: 99.5 us -> none  [the longest x1 57.2 us: body(): lax.all_gather(mlp_state[0, :, 0].astype(bf16), both, axis=0, tiled=True)]
    pallas_call x1, Pallas kernels: 37.9 us -> 48.9 us  [backward_attention(): pl.pallas_call(backward_kernel, in_specs=[SMEM] + [VMEM] * 11, out_specs=...]
  transfers between devices with their start and end apart: 5 -> 1, of which waited for: 5 -> 0; matrix products, arithmetic and copies ran while one was open for 5% -> 2% of each run, Pallas kernels for 8% -> 32%
where the time goes in v2:
time: 472 us; the launch traced here: 467 us
  Pallas kernels  413 us (88%)
  local copies, waits for them, and re-layouts  24 us (5%)
  other arithmetic  15.3 us (3%)
  between operations  14.5 us (3%)
    pallas_call x2, Pallas kernels, scatter_blocks(): pl.pallas_call(partial(scatter_kernel, n), in_specs=[VMEM], out_specs=VME...  91.2 us
    pallas_call x2, Pallas kernels, gather_blocks(): pl.pallas_call(partial(gather_kernel, n), in_specs=[VMEM], out_specs=VMEM...  90.2 us
    pallas_call x2, Pallas kernels, soap_update(): pl.pallas_call(soap_kernel, grid_spec=pltpu.PrefetchScalarGridSpec(num_sc...  57.3 us
    pallas_call x1, Pallas kernels, feed_forward(): pl.pallas_call(partial(mlp_kernel, parts, each), in_specs=[SMEM, VMEM, VM...  51 us
    pallas_call x1, Pallas kernels, backward_attention(): pl.pallas_call(backward_kernel, in_specs=[SMEM] + [VMEM] * 11, out_specs=...  48.9 us
    pallas_call x1, Pallas kernels, table_accumulate(): pl.pallas_call(accumulate_kernel, in_specs=[VMEM, VMEM], out_specs=VMEM,...  38.8 us
    pallas_call x1, Pallas kernels, forward_attention(): pl.pallas_call(forward_kernel, in_specs=[SMEM, VMEM, ANY, VMEM, VMEM], ou...  27.5 us
  transfers between devices with their start and end apart: 1, of which 0 were waited for; matrix products, arithmetic and copies ran while one was open for 2% of the time, Pallas kernels for 32%

profile of v2, /device:TPU:0, one launch (start us, length us, event | category | flops | bytes accessed | tf_op | source)
XLA Modules:
  0.0 467.2 jit_solution(9172217271378750266)
XLA Ops:
  7.2 0.0 all-reduce.7.cloned.1.call-start
  7.2 1.0 copy.46
  8.3 2.6 reshape.66
  10.9 1.7 fusion.1.own
  12.6 37.4 %gather0.1.slots = bf16[160,128,128]{2,1,0:T(8,128)(2,1)} custom-call(bf16[5,128,128]{2,1,0:T(8,128)(2,1)} %fusion.1.own), custom_call_target="tpu_custom_call" | custom-call | tf_op jit(solution)/shard_map/gather0/pallas_call | solution.py:362
  49.9 1.8 fusion.own
  51.8 52.9 %gather1.1.slots = bf16[288,128,128]{2,1,0:T(8,128)(2,1)} custom-call(bf16[9,128,128]{2,1,0:T(8,128)(2,1)} %fusion.own), custom_call_target="tpu_custom_call" | custom-call | tf_op jit(solution)/shard_map/gather1/pallas_call | solution.py:362
  104.7 7.8 %reduce = f32[788,768]{1,0:T(8,128)} reduce(f32[1,788,768]{2,0,1:T(1,128)S(1)} %copy-done.1, f32[]{:T(128)} %constant.74), dimensions={0}, to_apply=%param.14.reduce_sub_computation | reduce | bytes 4841476 | tf_op args[1]
  112.5 2.0 reshape.68
  114.4 0.6 pad.18.table_ref
  115.1 1.7 pad.19.cot
  116.8 0.7 pad.17.idx_ref
  117.5 8.3 %table_lookup.1.bias = f32[12,208,256]{2,1,0:T(8,128)} custom-call(s32[208,256]{1,0:T(8,128)} %pad.17.idx_ref, f32[12,768]{1,0:T(8,128)} %pad.18.table_ref), custom_call_target="tpu_custom_call" | custom-call | tf_op jit(solution)/shard_map/table_lookup/pallas_call | solution.py:426
  125.8 1.1 pad.16.tok
  126.9 27.5 %forward_attention.1 = (bf16[4,768,768]{2,1,0:T(8,128)(2,1)}, bf16[4,208,768]{2,1,0:T(8,128)(2,1)}, bf16[4,208,768]{2,1,0:T(8,128)(2,1)}, bf16[4,208,768]{2,1,0:...) custom-call(s32[144]{0:T(256)} %own.5, ...), custom_call_target="tpu_custom_call" | custom-call | tf_op jit(solution)/shard_map/forward_attention/pallas_call | solution.py:550
  154.4 51.0 %feed_forward.1 = (bf16[4,208,768]{2,1,0:T(8,128)(2,1)}, f32[4,208,768]{2,1,0:T(8,128)}, bf16[4,208,768]{2,1,0:T(8,128)(2,1)}, f32[8,768]{1,0:T(8,128)}, f32[1,3...) custom-call(s32[144]{0:T(256)} %own.4, f32[4,208,768]{2,1,0:T(8,128)} %get-tuple-element.32.mid, ...), custom_call_target="tpu_custom_call" | custom-call | tf_op jit(solution)/shard_map/feed_forward/pallas_call | solution.py:723
  205.4 48.9 %backward_attention.1 = (f32[4,208,768]{2,1,0:T(8,128)}, f32[12,208,256]{2,1,0:T(8,128)}, f32[8,768]{1,0:T(8,128)}, bf16[160,128,128]{2,1,0:T(8,128)(2,1)}) custom-call(s32[144]{0:T(256)} %own.5, bf16[4,208,768]{2,1,0:T(8,128)(2,1)} %pad.16.tok, bf16[4,768,768]{2,1,0:T(8,128)(2,1)} %get-tuple-element.36.w, bf16[4,208,768]{2,1,0:T(8,128)(2,1)} %get-tuple-element.37.q, ...), custom_call_target="tpu_custom_call" | custom-call | tf_op jit(solution)/shard_map/backward_attention/pallas_call | solution.py:859
  254.3 0.0 copy-start.9
  254.3 0.0 copy-start.8
  254.4 0.0 copy-start.5
  254.4 0.0 copy-start.10
  254.4 0.0 copy-start.11
  254.4 0.8 slice.45
  255.2 38.8 %table_accumulate.1 = f32[6,16,128]{2,1,0:T(8,128)} custom-call(f32[12,208,256]{2,1,0:T(8,128)} %get-tuple-element.53.grid_ref, s32[208,256]{1,0:T(8,128)} %pad.17.idx_ref), custom_call_target="tpu_custom_call" | custom-call | tf_op jit(solution)/shard_map/table_accumulate/pallas_call | solution.py:465
  294.0 1.4 copy_bitcast_fusion
  295.5 0.6 pad_maximum_fusion.2
  296.1 0.0 all-reduce.7.cloned.1.call-update
  296.2 0.1 fusion.16
  296.4 0.2 compare_reduce_fusion.1
  296.6 0.2 compare_reduce_fusion
  296.7 1.9 slice.44
  298.6 3.5 reshape.74
  302.1 36.7 %scatter3.1.grads = f32[5,128,128]{2,1,0:T(8,128)} custom-call(bf16[160,128,128]{2,1,0:T(8,128)(2,1)} %get-tuple-element.45.full), custom_call_target="tpu_custom_call" | custom-call | tf_op jit(solution)/shard_map/scatter3/pallas_call | solution.py:389
  338.8 0.5 convert_element_type.20.live
  339.3 54.5 %scatter2.1.grads = f32[9,128,128]{2,1,0:T(8,128)} custom-call(bf16[288,128,128]{2,1,0:T(8,128)(2,1)} %get-tuple-element.48.full), custom_call_target="tpu_custom_call" | custom-call | tf_op jit(solution)/shard_map/scatter2/pallas_call | solution.py:389
  393.8 0.6 convert_element_type.21.live
  394.4 0.1 slice.43
  394.5 1.3 reshape.69
  395.8 25.1 %soap.2 = (f32[5,5,128,128]{3,2,1,0:T(8,128)}, bf16[5,128,128]{2,1,0:T(8,128)(2,1)}) custom-call(s32[5]{0:T(128)} %convert_element_type.20.live, f32[5,128,128]{2,1,0:T(8,128)} %scatter3.1.grads, f32[5,7,128,128]{3,2,1,0:T(8,128)} %state.1), custom_call_target="tpu_custom_call" | custom-call | tf_op jit(solution)/shard_map/soap/pallas_call | solution.py:978
  421.0 32.2 %soap.3 = (f32[9,5,128,128]{3,2,1,0:T(8,128)}, bf16[9,128,128]{2,1,0:T(8,128)(2,1)}) custom-call(s32[9]{0:T(128)} %convert_element_type.21.live, f32[9,128,128]{2,1,0:T(8,128)} %scatter2.1.grads, f32[9,7,128,128]{3,2,1,0:T(8,128)} %bitcast.73), custom_call_target="tpu_custom_call" | custom-call | tf_op jit(solution)/shard_map/soap/pallas_call | solution.py:978
  453.1 0.8 subtract_bitcast_fusion
  454.0 0.8 pad_maximum_fusion.1
  454.8 0.8 copy.55
  455.6 0.8 subtract_bitcast_fusion.1
  456.4 0.8 pad_maximum_fusion
  457.2 0.7 copy.54
  458.0 0.7 divide_subtract_fusion
  458.7 1.4 pad_maximum_fusion.3
  (24 shorter events, 0.1 us)
Async XLA Ops:
  7.2 446.0 %all-reduce.7.cloned.1.call-start = ((), (), s32[]{:S(2)}) async-start(), calls=%async_computation | async-start | bytes 221184 | tf_op jit(solution)/shard_map/psum | solution.py:1075
  51.8 52.9 %copy-start.1 = (f32[1,788,768]{2,0,1:T(1,128)S(1)}, f32[1,788,768]{2,0,1:T(1,128)}, u32[]{:S(2)}) copy-start(f32[1,788,768]{2,0,1:T(1,128)} %param.14) | copy-start | bytes 7262212
  112.5 2.0 copy-start.4
  116.8 9.1 %copy-start = (bf16[4,197,768]{2,1,0:T(8,128)(2,1)S(1)}, bf16[4,197,768]{2,1,0:T(8,128)(2,1)}, u32[]{:S(2)}) copy-start(bf16[4,197,768]{2,1,0:T(8,128)(2,1)} %reshape.66) | copy-start | bytes 3631108
  254.3 41.1 %copy-start.9 = (f32[8,768]{1,0:T(8,128)S(1)}, f32[8,768]{1,0:T(8,128)}, u32[]{:S(2)}) copy-start(f32[8,768]{1,0:T(8,128)} %get-tuple-element.52) | copy-start | bytes 73732
  254.3 41.8 %copy-start.8 = (f32[2,3072]{1,0:T(2,128)S(1)}, f32[2,3072]{1,0:T(2,128)}, u32[]{:S(2)}) copy-start(f32[2,3072]{1,0:T(2,128)} %param.25) | copy-start | bytes 73732
  254.4 41.8 %copy-start.5 = (f32[2,12,732]{2,0,1:T(2,128)S(1)}, f32[2,12,732]{2,0,1:T(2,128)}, u32[]{:S(2)}) copy-start(f32[2,12,732]{2,0,1:T(2,128)} %param.23) | copy-start | bytes 210820
  254.4 41.9 %copy-start.6 = (f32[2,10,768]{2,0,1:T(2,128)S(1)}, f32[2,10,768]{2,0,1:T(2,128)}, u32[]{:S(2)}) copy-start(f32[2,10,768]{2,0,1:T(2,128)} %param.21) | copy-start | bytes 184324
  254.4 42.0 %copy-start.10 = (s32[144]{0:T(256)S(1)}, s32[144]{0:T(256)}, u32[]{:S(2)}) copy-start(s32[144]{0:T(256)} %own.5) | copy-start | bytes 1732
  254.4 42.2 %copy-start.11 = (s32[144]{0:T(256)S(1)}, s32[144]{0:T(256)}, u32[]{:S(2)}) copy-start(s32[144]{0:T(256)} %own.4) | copy-start | bytes 1732
  339.3 55.1 %copy-start.2 = (bf16[4,208,768]{2,1,0:T(8,128)(2,1)S(1)}, bf16[4,208,768]{2,1,0:T(8,128)(2,1)}, u32[]{:S(2)}) copy-start(bf16[4,208,768]{2,1,0:T(8,128)(2,1)} %get-tuple-element.35) | copy-start | bytes 3833860
  421.0 34.6 %copy-start.3 = (f32[10,768]{1,0:T(8,128)S(1)}, f32[10,768]{1,0:T(8,128)}, u32[]{:S(2)}) copy-start(f32[10,768]{1,0:T(8,128)} %vec.5) | copy-start | bytes 92164
  421.0 37.0 %copy-start.7 = (f32[3072]{0:T(1024)S(1)}, f32[3072]{0:T(1024)}, u32[]{:S(2)}) copy-start(f32[3072]{0:T(1024)} %param.24) | copy-start | bytes 36868
Sparse Core Ops, SparseCore 0:
  296.2 124.8 all-reduce.6
